TPU v7x, 256 devices: a whole 4x4x8 slice. The times are simulated.
256 devices in a mesh: layer: 32 (over x, z), row: 8 (over y, core).
Axes of the slice: x: 4, y: 4, z: 8, core: 2. Of those that a mesh axis runs over, the one named last changes fastest.
Arguments:
- leaf_rhs: bfloat16 [262144, 512], P(('layer', 'row')), may hold values from -3 to 3
- leaf_inv: bfloat16 [2048, 128, 128], P(('layer', 'row')), may hold values from -1 to 1.25, as said below
- coupling: bfloat16 [262144, 5, 128], P(('layer', 'row')), may hold values from -0.046875 to 0.046875
- pattern: int32 [2048, 5], P(('layer', 'row')), may hold values 0 or 1
- anc_rhs: float32 [32, 5, 1024, 512], P('layer', None, 'row'), may hold values from -2 to 2
- anc_blocks: bfloat16 [32, 15, 1024, 1024], P('layer', None, 'row'), may hold values from -1 to 1.25, as said below
Outputs:
- x_leaf: float32 [262144, 512], P(('layer', 'row'))
- x_anc: float32 [32, 5, 1024, 512], P('layer', None, 'row')
Inputs may be any that keep to these rules, and one draw needn't show every extreme that they name: `leaf_inv`: each block is lower triangular with a positive diagonal. For every level t and block index k of blk(s, t), the copies anc_blocks[l, k] are equal for all layers l of one group of 2 ** (t + 1) layers; the blocks blk(t, t) are lower triangular with a positive diagonal.
All inputs are finite; a program needn't handle non-finite values. No bound on the sum of `pattern` on one device may be relied on, other than what follows from the above.
Results may differ from a plain program's by a relative error of at most 0.009.
Values may be sent and summed in bfloat16 or wider, within the bound.
No kernel may reach another device: no remote copies, remote signals or barrier semaphores. Data moves between devices by JAX's collectives and lax.ppermute only.
A program may use at most 64 MiB of HBM per device.

v0:
```python
import jax
import jax.numpy as jnp
from jax import lax
from jax.sharding import PartitionSpec as P


def partner(value, axis, bit):
    mask = 2**bit
    pairs = [(source, source ^ mask) for source in range(lax.axis_size(axis))]
    return lax.ppermute(value, axis, pairs)


def block_start(tree_level, level_total):
    return tree_level * level_total - tree_level * (tree_level - 1) // 2


def body(leaf_rhs, leaf_inv, coupling, pattern, anc_rhs, anc_blocks):
    levels_here = anc_rhs.shape[1]
    supers = leaf_inv.shape[0]
    block_width = leaf_inv.shape[1]
    num_sides = leaf_rhs.shape[1]
    sep_rows = anc_rhs.shape[2]
    leaf_rows = supers * block_width
    layer_pos = lax.axis_index("layer")
    leaf_y = jnp.einsum(
        "kab,kbr->kar",
        leaf_inv,
        leaf_rhs.reshape(supers, block_width, num_sides),
        preferred_element_type=jnp.float32,
    )
    leaf_yb = leaf_y.astype(jnp.bfloat16).reshape(leaf_rows, num_sides)
    masked = (
        coupling.reshape(supers, block_width, levels_here, sep_rows)
        * pattern.astype(jnp.bfloat16)[:, None, :, None]
    )
    masked = masked.reshape(leaf_rows, levels_here * sep_rows)
    leaf_terms = lax.dot_general(
        masked, leaf_yb, (((0,), (0,)), ((), ())), preferred_element_type=jnp.float32
    )
    pending = anc_rhs[0] - leaf_terms.reshape(levels_here, sep_rows, num_sides)
    solved = []
    for tree_level in range(levels_here):
        first_block = block_start(tree_level, levels_here)
        block_count = levels_here - tree_level
        stacked = anc_blocks[0, first_block : first_block + block_count].reshape(
            block_count * sep_rows, -1
        )
        level_total = pending[tree_level]
        for bit_index in range(tree_level + 1):
            level_total = level_total + partner(level_total, "layer", bit_index)
        level_z = level_total.astype(jnp.bfloat16)

        def accumulate(running, shard_piece, first_row, stacked=stacked):
            return jnp.dot(stacked, shard_piece, preferred_element_type=jnp.float32)

        product = accumulate(
            jnp.zeros((block_count * sep_rows, num_sides), jnp.float32),
            lax.all_gather(level_z, "row", axis=0, tiled=True),
            jnp.int32(0),
        )
        solved.append(product[:sep_rows].astype(jnp.bfloat16))
        if block_count > 1:
            later_terms = product[sep_rows:].reshape(block_count - 1, sep_rows, num_sides)
            representative = (layer_pos % 2 ** (tree_level + 1) == 0).astype(jnp.float32)
            pending = pending.at[tree_level + 1 :].add(-representative * later_terms)
    answers = [None] * levels_here
    for tree_level in reversed(range(levels_here)):
        first_block = block_start(tree_level, levels_here)
        block_count = levels_here - tree_level
        stacked_vals = jnp.stack(
            [solved[tree_level]]
            + [-answers[above].astype(jnp.bfloat16) for above in range(tree_level + 1, levels_here)]
        )
        factor = anc_blocks[0, first_block : first_block + block_count]

        def transposed(first_row, row_count, factor=factor, stacked_vals=stacked_vals):
            return lax.dot_general(
                factor,
                stacked_vals,
                (((0, 1), (0, 1)), ((), ())),
                preferred_element_type=jnp.float32,
            )

        answers[tree_level] = lax.psum_scatter(
            transposed(jnp.int32(0), sep_rows * lax.axis_size("row")),
            "row",
            scatter_dimension=0,
            tiled=True,
        )
    anc_out = jnp.stack(answers)
    solved_bf = anc_out.astype(jnp.bfloat16).reshape(levels_here * sep_rows, num_sides)
    back_terms = jnp.dot(masked, solved_bf, preferred_element_type=jnp.float32)
    leaf_vb = (leaf_y.reshape(leaf_rows, num_sides) - back_terms).astype(jnp.bfloat16)
    x_leaf = jnp.einsum(
        "kba,kbr->kar",
        leaf_inv,
        leaf_vb.reshape(supers, block_width, num_sides),
        preferred_element_type=jnp.float32,
    )
    return (x_leaf.reshape(leaf_rows, num_sides), anc_out[None])


def solution(mesh):
    placed = (
        P(("layer", "row"), None),
        P(("layer", "row"), None, None),
        P(("layer", "row"), None, None),
        P(("layer", "row"), None),
        P("layer", None, "row", None),
        P("layer", None, "row", None),
    )
    return jax.shard_map(
        body,
        mesh=mesh,
        in_specs=placed,
        out_specs=(P(("layer", "row"), None), P("layer", None, "row", None)),
        check_vma=False,
    )
```

profile of v0, /device:TPU:1, one launch (start us, length us, event | category | flops | bytes accessed | tf_op | source)
XLA Modules:
  0.0 548.9 jit_solution(5028942331560647817)
XLA Ops:
  25.3 28.3 %all-gather.6.cloned.1.call-done = bf16[1024,512]{1,0:T(8,128)(2,1)} async-done(((bf16[128,512]{1,0:T(8,128)(2,1)}), bf16[1024,512]{1,0:T(8,128)(2,1)}) %all-gather.6.cloned.1.call-update) | async-done | bytes 1048592 | tf_op jit(solution)/shard_map/all_gather | solution.py:58
  59.6 6.4 %collective-permute-done.1 = f32[128,512]{1,0:T(8,128)S(1)} collective-permute-done((f32[128,512]{1,0:T(8,128)S(1)}, f32[128,512]{1,0:T(8,128)S(1)}, u32[]{:S(2)}, u32[]{:S(2)}) %collective-permute-start.1) | collective-permute-done | bytes 262176 | tf_op jit(solution)/shard_map/ppermute | solution.py:10
  68.3 11.4 %collective-permute-done.2 = f32[128,512]{1,0:T(8,128)S(1)} collective-permute-done((f32[128,512]{1,0:T(8,128)S(1)}, f32[128,512]{1,0:T(8,128)S(1)}, u32[]{:S(2)}, u32[]{:S(2)}) %collective-permute-start.2) | collective-permute-done | bytes 262176 | tf_op jit(solution)/shard_map/ppermute | solution.py:10
  82.8 24.9 %all-gather.8.cloned.1.call-done = bf16[1024,512]{1,0:T(8,128)(2,1)} async-done(((bf16[128,512]{1,0:T(8,128)(2,1)}), bf16[1024,512]{1,0:T(8,128)(2,1)}) %all-gather.8.cloned.1.call-update) | async-done | bytes 1048592 | tf_op jit(solution)/shard_map/all_gather | solution.py:58
  121.9 11.4 %collective-permute-done.4 = f32[128,512]{1,0:T(8,128)S(1)} collective-permute-done((f32[128,512]{1,0:T(8,128)S(1)}, f32[128,512]{1,0:T(8,128)S(1)}, u32[]{:S(2)}, u32[]{:S(2)}) %collective-permute-start.4) | collective-permute-done | bytes 262176 | tf_op jit(solution)/shard_map/ppermute | solution.py:10
  133.3 6.5 %collective-permute-start.5 = (f32[128,512]{1,0:T(8,128)S(1)}, f32[128,512]{1,0:T(8,128)S(1)}, u32[]{:S(2)}, u32[]{:S(2)}) collective-permute-start(f32[128,512]{1,0:T(8,128)S(1)} %add.104), channel_id=1, source_target_pairs={{0,32},{8,40},{16,48},{24,56},{32,0},{40,8},{48,16},{56,24},{64,96... | collective-permute-start | bytes 786440 | tf_op jit(solution)/shard_map/ppermute | solution.py:10
  139.9 8.8 %collective-permute-done.5 = f32[128,512]{1,0:T(8,128)S(1)} collective-permute-done((f32[128,512]{1,0:T(8,128)S(1)}, f32[128,512]{1,0:T(8,128)S(1)}, u32[]{:S(2)}, u32[]{:S(2)}) %collective-permute-start.5) | collective-permute-done | bytes 262176 | tf_op jit(solution)/shard_map/ppermute | solution.py:10
  151.5 24.7 %all-gather.10.cloned.1.call-done = bf16[1024,512]{1,0:T(8,128)(2,1)} async-done(((bf16[128,512]{1,0:T(8,128)(2,1)}), bf16[1024,512]{1,0:T(8,128)(2,1)}) %all-gather.10.cloned.1.call-update) | async-done | bytes 1048592 | tf_op jit(solution)/shard_map/all_gather | solution.py:58
  180.7 6.4 %collective-permute-done.6 = f32[128,512]{1,0:T(8,128)S(1)} collective-permute-done((f32[128,512]{1,0:T(8,128)S(1)}, f32[128,512]{1,0:T(8,128)S(1)}, u32[]{:S(2)}, u32[]{:S(2)}) %collective-permute-start.6) | collective-permute-done | bytes 262176 | tf_op jit(solution)/shard_map/ppermute | solution.py:10
  189.4 11.4 %collective-permute-done.7 = f32[128,512]{1,0:T(8,128)S(1)} collective-permute-done((f32[128,512]{1,0:T(8,128)S(1)}, f32[128,512]{1,0:T(8,128)S(1)}, u32[]{:S(2)}, u32[]{:S(2)}) %collective-permute-start.7) | collective-permute-done | bytes 262176 | tf_op jit(solution)/shard_map/ppermute | solution.py:10
  200.9 6.5 %collective-permute-start.8 = (f32[128,512]{1,0:T(8,128)S(1)}, f32[128,512]{1,0:T(8,128)S(1)}, u32[]{:S(2)}, u32[]{:S(2)}) collective-permute-start(f32[128,512]{1,0:T(8,128)S(1)} %add.109), channel_id=1, source_target_pairs={{0,32},{8,40},{16,48},{24,56},{32,0},{40,8},{48,16},{56,24},{64,96... | collective-permute-start | bytes 786440 | tf_op jit(solution)/shard_map/ppermute | solution.py:10
  207.4 8.8 %collective-permute-done.8 = f32[128,512]{1,0:T(8,128)S(1)} collective-permute-done((f32[128,512]{1,0:T(8,128)S(1)}, f32[128,512]{1,0:T(8,128)S(1)}, u32[]{:S(2)}, u32[]{:S(2)}) %collective-permute-start.8) | collective-permute-done | bytes 262176 | tf_op jit(solution)/shard_map/ppermute | solution.py:10
  224.2 27.4 %all-gather.12.cloned.1.call-done = bf16[1024,512]{1,0:T(8,128)(2,1)} async-done(((bf16[128,512]{1,0:T(8,128)(2,1)}), bf16[1024,512]{1,0:T(8,128)(2,1)}) %all-gather.12.cloned.1.call-update) | async-done | bytes 1048592 | tf_op jit(solution)/shard_map/all_gather | solution.py:58
  254.9 6.4 %collective-permute-done.10 = f32[128,512]{1,0:T(8,128)S(1)} collective-permute-done((f32[128,512]{1,0:T(8,128)S(1)}, f32[128,512]{1,0:T(8,128)S(1)}, u32[]{:S(2)}, u32[]{:S(2)}) %collective-permute-start.10) | collective-permute-done | bytes 262176 | tf_op jit(solution)/shard_map/ppermute | solution.py:10
  263.7 11.4 %collective-permute-done.11 = f32[128,512]{1,0:T(8,128)S(1)} collective-permute-done((f32[128,512]{1,0:T(8,128)S(1)}, f32[128,512]{1,0:T(8,128)S(1)}, u32[]{:S(2)}, u32[]{:S(2)}) %collective-permute-start.11) | collective-permute-done | bytes 262176 | tf_op jit(solution)/shard_map/ppermute | solution.py:10
  275.2 6.7 %collective-permute-start.12 = (f32[128,512]{1,0:T(8,128)S(1)}, f32[128,512]{1,0:T(8,128)S(1)}, u32[]{:S(2)}, u32[]{:S(2)}) collective-permute-start(f32[128,512]{1,0:T(8,128)S(1)} %add.115), channel_id=1, source_target_pairs={{0,32},{8,40},{16,48},{24,56},{32,0},{40,8},{48,16},{56,24},{64,96... | collective-permute-start | bytes 786440 | tf_op jit(solution)/shard_map/ppermute | solution.py:10
  281.8 8.8 %collective-permute-done.12 = f32[128,512]{1,0:T(8,128)S(1)} collective-permute-done((f32[128,512]{1,0:T(8,128)S(1)}, f32[128,512]{1,0:T(8,128)S(1)}, u32[]{:S(2)}, u32[]{:S(2)}) %collective-permute-start.12) | collective-permute-done | bytes 262176 | tf_op jit(solution)/shard_map/ppermute | solution.py:10
  298.9 6.7 %collective-permute-done.14 = f32[128,512]{1,0:T(8,128)S(1)} collective-permute-done((f32[128,512]{1,0:T(8,128)S(1)}, f32[128,512]{1,0:T(8,128)S(1)}, u32[]{:S(2)}, u32[]{:S(2)}) %collective-permute-start.14) | collective-permute-done | bytes 262176 | tf_op jit(solution)/shard_map/ppermute | solution.py:10
  306.3 28.8 %all-gather.14.cloned.1.call-done = bf16[1024,512]{1,0:T(8,128)(2,1)} async-done(((bf16[128,512]{1,0:T(8,128)(2,1)}), bf16[1024,512]{1,0:T(8,128)(2,1)}) %all-gather.14.cloned.1.call-update) | async-done | bytes 1048592 | tf_op jit(solution)/shard_map/all_gather | solution.py:58
  340.1 32.1 %reduce-scatter.6.cloned.1.call-done = f32[128,512]{1,0:T(8,128)} async-done(((f32[1024,512]{1,0:T(8,128)}), f32[128,512]{1,0:T(8,128)}) %reduce-scatter.6.cloned.1.call-update) | async-done | bytes 262160 | tf_op jit(solution)/shard_map/reduce_scatter | solution.py:84
  377.0 34.2 %reduce-scatter.8.cloned.1.call-done = f32[128,512]{1,0:T(8,128)} async-done(((f32[1024,512]{1,0:T(8,128)}), f32[128,512]{1,0:T(8,128)}) %reduce-scatter.8.cloned.1.call-update) | async-done | bytes 262160 | tf_op jit(solution)/shard_map/reduce_scatter | solution.py:84
  416.4 34.2 %reduce-scatter.10.cloned.1.call-done = f32[128,512]{1,0:T(8,128)} async-done(((f32[1024,512]{1,0:T(8,128)}), f32[128,512]{1,0:T(8,128)}) %reduce-scatter.10.cloned.1.call-update) | async-done | bytes 262160 | tf_op jit(solution)/shard_map/reduce_scatter | solution.py:84
  456.6 33.5 %reduce-scatter.12.cloned.1.call-done = f32[128,512]{1,0:T(8,128)} async-done(((f32[1024,512]{1,0:T(8,128)}), f32[128,512]{1,0:T(8,128)}) %reduce-scatter.12.cloned.1.call-update) | async-done | bytes 262160 | tf_op jit(solution)/shard_map/reduce_scatter | solution.py:84
  499.6 35.1 %reduce-scatter.14.cloned.1.call-done = f32[128,512]{1,0:T(8,128)} async-done(((f32[1024,512]{1,0:T(8,128)}), f32[128,512]{1,0:T(8,128)}) %reduce-scatter.14.cloned.1.call-update) | async-done | bytes 262160 | tf_op jit(solution)/shard_map/reduce_scatter | solution.py:84
  (142 shorter events, 113.4 us)
Async XLA Ops:
  7.2 46.5 %all-gather.6.cloned.1.call-start = ((), (), s32[]{:S(2)}) async-start(), calls=%async_computation.5 | async-start | bytes 1179648 | tf_op jit(solution)/shard_map/all_gather | solution.py:58
  14.5 7.5 %collective-permute-start = (f32[128,512]{1,0:T(8,128)S(1)}, f32[128,512]{1,0:T(8,128)S(1)}, u32[]{:S(2)}, u32[]{:S(2)}) collective-permute-start(f32[128,512]{1,0:T(8,128)S(1)} %slice_bitcast_fusion.3), channel_id=1, source_target_pairs={{0,8},{8,0},{16,24},{24,16},{32,40},{40,32},{48,56},{56,48},{64,72... | collective-permute-start | bytes 786440 | tf_op jit(solution)/shard_map/ppermute | solution.py:10
  22.8 84.9 %all-gather.8.cloned.1.call-start = ((), (), s32[]{:S(2)}) async-start(), calls=%async_computation.6 | async-start | bytes 1179648 | tf_op jit(solution)/shard_map/all_gather | solution.py:58
  58.2 7.8 %collective-permute-start.1 = (f32[128,512]{1,0:T(8,128)S(1)}, f32[128,512]{1,0:T(8,128)S(1)}, u32[]{:S(2)}, u32[]{:S(2)}) collective-permute-start(f32[128,512]{1,0:T(8,128)S(1)} %slice_bitcast_fusion.2), channel_id=1, source_target_pairs={{0,8},{8,0},{16,24},{24,16},{32,40},{40,32},{48,56},{56,48},{64,72... | collective-permute-start | bytes 786440 | tf_op jit(solution)/shard_map/ppermute | solution.py:10
  66.0 13.8 %collective-permute-start.2 = (f32[128,512]{1,0:T(8,128)S(1)}, f32[128,512]{1,0:T(8,128)S(1)}, u32[]{:S(2)}, u32[]{:S(2)}) collective-permute-start(f32[128,512]{1,0:T(8,128)S(1)} %fusion.38), channel_id=1, source_target_pairs={{0,16},{8,24},{16,0},{24,8},{32,48},{40,56},{48,32},{56,40},{64,80... | collective-permute-start | bytes 786440 | tf_op jit(solution)/shard_map/ppermute | solution.py:10
  80.5 95.8 %all-gather.10.cloned.1.call-start = ((), (), s32[]{:S(2)}) async-start(), calls=%async_computation.7 | async-start | bytes 1179648 | tf_op jit(solution)/shard_map/all_gather | solution.py:58
  111.7 7.8 %collective-permute-start.3 = (f32[128,512]{1,0:T(8,128)S(1)}, f32[128,512]{1,0:T(8,128)S(1)}, u32[]{:S(2)}, u32[]{:S(2)}) collective-permute-start(f32[128,512]{1,0:T(8,128)S(1)} %slice_bitcast_fusion.1), channel_id=1, source_target_pairs={{0,8},{8,0},{16,24},{24,16},{32,40},{40,32},{48,56},{56,48},{64,72... | collective-permute-start | bytes 786440 | tf_op jit(solution)/shard_map/ppermute | solution.py:10
  119.5 13.8 %collective-permute-start.4 = (f32[128,512]{1,0:T(8,128)S(1)}, f32[128,512]{1,0:T(8,128)S(1)}, u32[]{:S(2)}, u32[]{:S(2)}) collective-permute-start(f32[128,512]{1,0:T(8,128)S(1)} %fusion.39), channel_id=1, source_target_pairs={{0,16},{8,24},{16,0},{24,8},{32,48},{40,56},{48,32},{56,40},{64,80... | collective-permute-start | bytes 786440 | tf_op jit(solution)/shard_map/ppermute | solution.py:10
  133.3 15.4 %collective-permute-start.5 = (f32[128,512]{1,0:T(8,128)S(1)}, f32[128,512]{1,0:T(8,128)S(1)}, u32[]{:S(2)}, u32[]{:S(2)}) collective-permute-start(f32[128,512]{1,0:T(8,128)S(1)} %add.104), channel_id=1, source_target_pairs={{0,32},{8,40},{16,48},{24,56},{32,0},{40,8},{48,16},{56,24},{64,96... | collective-permute-start | bytes 786440 | tf_op jit(solution)/shard_map/ppermute | solution.py:10
  149.4 102.2 %all-gather.12.cloned.1.call-start = ((), (), s32[]{:S(2)}) async-start(), calls=%async_computation.8 | async-start | bytes 1179648 | tf_op jit(solution)/shard_map/all_gather | solution.py:58
  179.3 7.8 %collective-permute-start.6 = (f32[128,512]{1,0:T(8,128)S(1)}, f32[128,512]{1,0:T(8,128)S(1)}, u32[]{:S(2)}, u32[]{:S(2)}) collective-permute-start(f32[128,512]{1,0:T(8,128)S(1)} %slice_bitcast_fusion), channel_id=1, source_target_pairs={{0,8},{8,0},{16,24},{24,16},{32,40},{40,32},{48,56},{56,48},{64,72... | collective-permute-start | bytes 786440 | tf_op jit(solution)/shard_map/ppermute | solution.py:10
  187.1 13.8 %collective-permute-start.7 = (f32[128,512]{1,0:T(8,128)S(1)}, f32[128,512]{1,0:T(8,128)S(1)}, u32[]{:S(2)}, u32[]{:S(2)}) collective-permute-start(f32[128,512]{1,0:T(8,128)S(1)} %fusion.40), channel_id=1, source_target_pairs={{0,16},{8,24},{16,0},{24,8},{32,48},{40,56},{48,32},{56,40},{64,80... | collective-permute-start | bytes 786440 | tf_op jit(solution)/shard_map/ppermute | solution.py:10
  200.9 15.3 %collective-permute-start.8 = (f32[128,512]{1,0:T(8,128)S(1)}, f32[128,512]{1,0:T(8,128)S(1)}, u32[]{:S(2)}, u32[]{:S(2)}) collective-permute-start(f32[128,512]{1,0:T(8,128)S(1)} %add.109), channel_id=1, source_target_pairs={{0,32},{8,40},{16,48},{24,56},{32,0},{40,8},{48,16},{56,24},{64,96... | collective-permute-start | bytes 786440 | tf_op jit(solution)/shard_map/ppermute | solution.py:10
  216.3 5.3 collective-permute-start.9
  222.3 112.7 %all-gather.14.cloned.1.call-start = ((), (), s32[]{:S(2)}) async-start(), calls=%async_computation.9 | async-start | bytes 1179648 | tf_op jit(solution)/shard_map/all_gather | solution.py:58
  253.5 7.8 %collective-permute-start.10 = (f32[128,512]{1,0:T(8,128)S(1)}, f32[128,512]{1,0:T(8,128)S(1)}, u32[]{:S(2)}, u32[]{:S(2)}) collective-permute-start(f32[128,512]{1,0:T(8,128)S(1)} %fusion.22), channel_id=1, source_target_pairs={{0,8},{8,0},{16,24},{24,16},{32,40},{40,32},{48,56},{56,48},{64,72... | collective-permute-start | bytes 786440 | tf_op jit(solution)/shard_map/ppermute | solution.py:10
  261.3 13.8 %collective-permute-start.11 = (f32[128,512]{1,0:T(8,128)S(1)}, f32[128,512]{1,0:T(8,128)S(1)}, u32[]{:S(2)}, u32[]{:S(2)}) collective-permute-start(f32[128,512]{1,0:T(8,128)S(1)} %add.114), channel_id=1, source_target_pairs={{0,16},{8,24},{16,0},{24,8},{32,48},{40,56},{48,32},{56,40},{64,80... | collective-permute-start | bytes 786440 | tf_op jit(solution)/shard_map/ppermute | solution.py:10
  275.2 15.5 %collective-permute-start.12 = (f32[128,512]{1,0:T(8,128)S(1)}, f32[128,512]{1,0:T(8,128)S(1)}, u32[]{:S(2)}, u32[]{:S(2)}) collective-permute-start(f32[128,512]{1,0:T(8,128)S(1)} %add.115), channel_id=1, source_target_pairs={{0,32},{8,40},{16,48},{24,56},{32,0},{40,8},{48,16},{56,24},{64,96... | collective-permute-start | bytes 786440 | tf_op jit(solution)/shard_map/ppermute | solution.py:10
  296.1 9.4 %collective-permute-start.14 = (f32[128,512]{1,0:T(8,128)S(1)}, f32[128,512]{1,0:T(8,128)S(1)}, u32[]{:S(2)}, u32[]{:S(2)}) collective-permute-start(f32[128,512]{1,0:T(8,128)S(1)} %add.117), channel_id=1, source_target_pairs={{0,128},{8,136},{16,144},{24,152},{32,160},{40,168},{48,176},{56,1... | collective-permute-start | bytes 786440 | tf_op jit(solution)/shard_map/ppermute | solution.py:10
  306.2 65.9 %reduce-scatter.6.cloned.1.call-start = ((), (), s32[]{:S(2)}) async-start(), calls=%async_computation.10 | async-start | bytes 2359296 | tf_op jit(solution)/shard_map/reduce_scatter | solution.py:84
  339.0 72.2 %reduce-scatter.8.cloned.1.call-start = ((), (), s32[]{:S(2)}) async-start(), calls=%async_computation.11 | async-start | bytes 2359296 | tf_op jit(solution)/shard_map/reduce_scatter | solution.py:84
  376.0 74.6 %reduce-scatter.10.cloned.1.call-start = ((), (), s32[]{:S(2)}) async-start(), calls=%async_computation.12 | async-start | bytes 2359296 | tf_op jit(solution)/shard_map/reduce_scatter | solution.py:84
  415.4 74.7 %reduce-scatter.12.cloned.1.call-start = ((), (), s32[]{:S(2)}) async-start(), calls=%async_computation.13 | async-start | bytes 2359296 | tf_op jit(solution)/shard_map/reduce_scatter | solution.py:84
  454.9 79.8 %reduce-scatter.14.cloned.1.call-start = ((), (), s32[]{:S(2)}) async-start(), calls=%async_computation.14 | async-start | bytes 2359296 | tf_op jit(solution)/shard_map/reduce_scatter | solution.py:84
  (21 other events, 169.5 us)
Sparse Core Ops, SparseCore 0:
  22.9 30.7 all-gather.5
  80.6 27.0 all-gather.7
  149.5 26.6 all-gather.9
  222.4 29.1 all-gather.11
  306.4 28.6 all-gather.13
  339.2 32.9 reduce-scatter.5
  376.1 35.0 reduce-scatter.7
  415.5 35.0 reduce-scatter.9
  455.0 35.0 reduce-scatter.11
  499.6 35.0 reduce-scatter.13
where the time goes:
time: 552 us; the launch traced here: 549 us
  waiting for transfers between devices  421 us (76%)
  starting transfers between devices  42.9 us (8%)
  matrix products  30.4 us (6%)
  local copies, waits for them, and re-layouts  26.3 us (5%)
  between operations  14.6 us (3%)
  other arithmetic  13.9 us (3%)
    reduce_scatter x5, waiting for transfers between devices, body(): lax.psum_scatter(transposed(jnp.int32(0), sep_rows * lax.axis_size('row')...  169 us
    all_gather x5, waiting for transfers between devices, body(): lax.all_gather(level_z, 'row', axis=0, tiled=True)  134 us
    ppermute x15, waiting for transfers between devices, partner(): return lax.ppermute(value, axis, pairs)  117 us
    ppermute x15, starting transfers between devices, partner(): return lax.ppermute(value, axis, pairs)  42.4 us
    dot_general x5, matrix products, transposed(): lax.dot_general(factor, stacked_vals, (((0, 1), (0, 1)), ((), ())), prefe...  17.2 us
    unnamed x48, local copies, waits for them, and re-layouts  14.3 us
  transfers between devices with their start and end apart: 25, of which 25 were waited for; matrix products, arithmetic and copies ran while one was open for 2% of the time, Pallas kernels for 0%

commit v1 on v0

v1 whole, which is shorter than its diff:
```python
import jax
import jax.numpy as jnp
from jax import lax
from jax.sharding import PartitionSpec as P


def swap_pairs(value, axis, bit):
    mask = 2**bit
    pairs = [(source, source ^ mask) for source in range(lax.axis_size(axis))]
    return lax.ppermute(value, axis, pairs)


def pair_groups(bit, layers, rows):
    groups = []
    for low in range(layers):
        if low >> bit & 1:
            continue
        groups.append(
            [low * rows + r for r in range(rows)] + [(low ^ (1 << bit)) * rows + r for r in range(rows)]
        )
    return groups


def exchange(payload, bit):
    groups = pair_groups(bit, lax.axis_size("layer"), lax.axis_size("row"))
    return lax.all_to_all(payload, ("layer", "row"), 0, 0, axis_index_groups=groups)


def block_start(tree_level, level_total):
    return tree_level * level_total - tree_level * (tree_level - 1) // 2


def body(leaf_rhs, leaf_inv, coupling, pattern, anc_rhs, anc_blocks):
    levels_here = anc_rhs.shape[1]
    supers = leaf_inv.shape[0]
    block_width = leaf_inv.shape[1]
    num_sides = leaf_rhs.shape[1]
    sep_rows = anc_rhs.shape[2]
    leaf_rows = supers * block_width
    row_count = lax.axis_size("row")
    layer_pos = lax.axis_index("layer")
    leaf_y = jnp.einsum(
        "kab,kbr->kar",
        leaf_inv,
        leaf_rhs.reshape(supers, block_width, num_sides),
        preferred_element_type=jnp.float32,
    )
    leaf_yb = leaf_y.astype(jnp.bfloat16).reshape(leaf_rows, num_sides)
    masked = (
        coupling.reshape(supers, block_width, levels_here, sep_rows)
        * pattern.astype(jnp.bfloat16)[:, None, :, None]
    )
    masked = masked.reshape(leaf_rows, levels_here * sep_rows)
    leaf_terms = lax.dot_general(
        masked, leaf_yb, (((0,), (0,)), ((), ())), preferred_element_type=jnp.float32
    )
    pending = anc_rhs[0] - leaf_terms.reshape(levels_here, sep_rows, num_sides)
    solved = []
    width = num_sides
    for tree_level in range(levels_here):
        first_block = block_start(tree_level, levels_here)
        block_count = levels_here - tree_level
        stacked = anc_blocks[0, first_block : first_block + block_count].reshape(
            block_count * sep_rows, -1
        )
        upper = (layer_pos >> tree_level & 1) == 1
        half = width // 2
        wire = jnp.bfloat16 if tree_level < 2 else jnp.float32
        if block_count > 1:
            low, high = pending[1:, :, :half], pending[1:, :, half:]
            kept = jnp.where(upper, high, low)
            sent = jnp.where(upper, low, high)
            got = swap_pairs(sent.astype(wire), "layer", tree_level)
        mine = pending[0].astype(wire)
        payload = jnp.stack([mine[:, :half], mine[:, half:]])
        payload = jnp.broadcast_to(payload[:, None], (2, row_count, sep_rows, half))
        pieces = exchange(payload.reshape(2 * row_count, sep_rows, half), tree_level)
        pieces = pieces.reshape(2, row_count * sep_rows, half).astype(jnp.float32)
        level_z = (pieces[0] + pieces[1]).astype(jnp.bfloat16)
        product = jnp.dot(stacked, level_z, preferred_element_type=jnp.float32)
        solved.append(product[:sep_rows].astype(jnp.bfloat16))
        if block_count > 1:
            later_terms = product[sep_rows:].reshape(block_count - 1, sep_rows, half)
            pending = kept + got.astype(jnp.float32) - later_terms
        width = half
    answers = None
    for tree_level in reversed(range(levels_here)):
        first_block = block_start(tree_level, levels_here)
        block_count = levels_here - tree_level
        upper = (layer_pos >> tree_level & 1) == 1
        wire = jnp.bfloat16 if tree_level < 2 else jnp.float32
        factor = anc_blocks[0, first_block : first_block + block_count]
        stacked_vals = solved[tree_level][None]
        if answers is not None:
            answers_b = answers.astype(jnp.bfloat16)
            got = swap_pairs(answers_b if wire == jnp.bfloat16 else answers, "layer", tree_level)
            stacked_vals = jnp.concatenate([stacked_vals, -answers_b])
        partial = lax.dot_general(
            factor,
            stacked_vals,
            (((0, 1), (0, 1)), ((), ())),
            preferred_element_type=jnp.float32,
        )
        partial = partial.astype(wire).reshape(1, row_count, sep_rows, width)
        payload = jnp.broadcast_to(partial, (2, row_count, sep_rows, width))
        pieces = exchange(payload.reshape(2 * row_count, sep_rows, width), tree_level)
        pieces = pieces.reshape(2, row_count, sep_rows, width).astype(jnp.float32).sum(axis=1)
        fresh = jnp.concatenate([pieces[0], pieces[1]], axis=-1)[None]
        if answers is not None:
            got = got.astype(jnp.float32)
            low = jnp.where(upper, got, answers)
            high = jnp.where(upper, answers, got)
            fresh = jnp.concatenate([fresh, jnp.concatenate([low, high], axis=-1)])
        answers = fresh
        width = 2 * width
    anc_out = answers
    solved_bf = anc_out.astype(jnp.bfloat16).reshape(levels_here * sep_rows, num_sides)
    back_terms = jnp.dot(masked, solved_bf, preferred_element_type=jnp.float32)
    leaf_vb = (leaf_y.reshape(leaf_rows, num_sides) - back_terms).astype(jnp.bfloat16)
    x_leaf = jnp.einsum(
        "kba,kbr->kar",
        leaf_inv,
        leaf_vb.reshape(supers, block_width, num_sides),
        preferred_element_type=jnp.float32,
    )
    return (x_leaf.reshape(leaf_rows, num_sides), anc_out[None])


def solution(mesh):
    placed = (
        P(("layer", "row"), None),
        P(("layer", "row"), None, None),
        P(("layer", "row"), None, None),
        P(("layer", "row"), None),
        P("layer", None, "row", None),
        P("layer", None, "row", None),
    )
    return jax.shard_map(
        body,
        mesh=mesh,
        in_specs=placed,
        out_specs=(P(("layer", "row"), None), P("layer", None, "row", None)),
        check_vma=False,
    )
```

time: 552 us -> 243 us (0.44)
  waiting for transfers between devices: 421 us -> 115 us
  starting transfers between devices: 42.9 us -> 81.3 us
  matrix products: 30.4 us -> 14.5 us
  between operations: 14.6 us -> 1.25 us
  local copies, waits for them, and re-layouts: 26.3 us -> 18.8 us
    reduce_scatter x5 -> x0, waiting for transfers between devices: 169 us -> none  [body(): lax.psum_scatter(transposed(jnp.int32(0), sep_rows * lax.axis_size('row')...]
    all_gather x5 -> x0, waiting for transfers between devices: 134 us -> none  [body(): lax.all_gather(level_z, 'row', axis=0, tiled=True)]
    ppermute x15 -> x8, waiting for transfers between devices: 117 us -> 51.1 us  [swap_pairs(): return lax.ppermute(value, axis, pairs)]
    all_to_all x0 -> x10, waiting for transfers between devices: none -> 63.6 us  [exchange(): lax.all_to_all(payload, ('layer', 'row'), 0, 0, axis_index_groups=groups)]
    all_to_all x0 -> x10, starting transfers between devices: none -> 60.3 us  [exchange(): lax.all_to_all(payload, ('layer', 'row'), 0, 0, axis_index_groups=groups)]
    ppermute x15 -> x8, starting transfers between devices: 42.4 us -> 20.9 us  [swap_pairs(): return lax.ppermute(value, axis, pairs)]
    dot_general x9, matrix products: 25.9 us -> 9.08 us  [the longest x5 7.5 us: body(): lax.dot_general(factor, stacked_vals, (((0, 1), (0, 1)), ((), ())), prefe...]
    broadcast_in_dim x0 -> x19, local copies, waits for them, and re-layouts: none -> 10.6 us  [the longest x9 4.67 us: body(): payload = jnp.broadcast_to(partial, (2, row_count, sep_rows, width))]
  transfers between devices with their start and end apart: 25 -> 18, of which waited for: 25 -> 13; matrix products, arithmetic and copies ran while one was open for 2% -> 4% of each run, Pallas kernels for 0% -> 0%
where the time goes in v1:
time: 243 us; the launch traced here: 242 us
  waiting for transfers between devices  115 us (47%)
  starting transfers between devices  81.3 us (33%)
  local copies, waits for them, and re-layouts  18.8 us (8%)
  matrix products  14.5 us (6%)
  other arithmetic  11 us (5%)
    all_to_all x10, waiting for transfers between devices, exchange(): lax.all_to_all(payload, ('layer', 'row'), 0, 0, axis_index_groups=groups)  63.6 us
    all_to_all x10, starting transfers between devices, exchange(): lax.all_to_all(payload, ('layer', 'row'), 0, 0, axis_index_groups=groups)  60.3 us
    ppermute x8, waiting for transfers between devices, swap_pairs(): return lax.ppermute(value, axis, pairs)  51.1 us
    ppermute x8, starting transfers between devices, swap_pairs(): return lax.ppermute(value, axis, pairs)  20.9 us
    dot_general x5, matrix products, body(): lax.dot_general(factor, stacked_vals, (((0, 1), (0, 1)), ((), ())), prefe...  7.5 us
  transfers between devices with their start and end apart: 18, of which 13 were waited for; matrix products, arithmetic and copies ran while one was open for 4% of the time, Pallas kernels for 0%

profile of v1, /device:TPU:1, one launch (start us, length us, event | category | flops | bytes accessed | tf_op | source)
XLA Modules:
  0.0 241.5 jit_solution(2478951884732236119)
XLA Ops:
  8.2 7.3 %all-to-all-start = ((bf16[16,128,256]{2,1,0:T(8,128)(2,1)}), bf16[16,128,256]{2,1,0:T(8,128)(2,1)S(1)}, u32[]{:S(2)}, u32[]{:S(2)}) async-start(bf16[16,128,256]{2,1,0:T(8,128)(2,1)} %bitcast.254), calls=%async_computation | async-start | bytes 2097152 | tf_op jit(solution)/shard_map/all_to_all | solution.py:26
  17.7 13.7 %all-to-all-done = bf16[16,128,256]{2,1,0:T(8,128)(2,1)S(1)} async-done(((bf16[16,128,256]{2,1,0:T(8,128)(2,1)}), bf16[16,128,256]{2,1,0:T(8,128)(2,1)S(1)}, u32[]{:S(2)}, u32[]{:S(2)}) %all-to-all-start) | async-done | bytes 1048608 | tf_op jit(solution)/shard_map/all_to_all | solution.py:26
  37.0 7.8 %all-to-all-start.1 = ((bf16[16,128,128]{2,1,0:T(8,128)(2,1)}), bf16[16,128,128]{2,1,0:T(8,128)(2,1)}, u32[]{:S(2)}, u32[]{:S(2)}) async-start(bf16[16,128,128]{2,1,0:T(8,128)(2,1)} %bitcast.20), calls=%async_computation.1 | async-start | bytes 1048576 | tf_op jit(solution)/shard_map/all_to_all | solution.py:26
  45.5 2.3 collective-permute-start.1
  47.8 16.3 %all-to-all-done.1 = bf16[16,128,128]{2,1,0:T(8,128)(2,1)} async-done(((bf16[16,128,128]{2,1,0:T(8,128)(2,1)}), bf16[16,128,128]{2,1,0:T(8,128)(2,1)}, u32[]{:S(2)}, u32[]{:S(2)}) %all-to-all-start.1) | async-done | bytes 524320 | tf_op jit(solution)/shard_map/all_to_all | solution.py:26
  67.7 7.2 %all-to-all-start.2 = ((f32[16,128,64]{1,2,0:T(8,128)}), f32[16,128,64]{1,2,0:T(8,128)S(1)}, u32[]{:S(2)}, u32[]{:S(2)}) async-start(f32[16,128,64]{1,2,0:T(8,128)} %bitcast.29), calls=%async_computation.2 | async-start | bytes 1048576 | tf_op jit(solution)/shard_map/all_to_all | solution.py:26
  75.7 5.3 %collective-permute-start.2 = (f32[2,128,64]{2,1,0:T(8,128)}, f32[2,128,64]{2,1,0:T(8,128)}, u32[]{:S(2)}, u32[]{:S(2)}) collective-permute-start(f32[2,128,64]{2,1,0:T(8,128)} %slice_select_fusion), channel_id=1, source_target_pairs={{0,32},{8,40},{16,48},{24,56},{32,0},{40,8},{48,16},{56,24},{64,96... | collective-permute-start | bytes 196616 | tf_op jit(solution)/shard_map/ppermute | solution.py:10
  81.0 13.3 %all-to-all-done.2 = f32[16,128,64]{1,2,0:T(8,128)S(1)} async-done(((f32[16,128,64]{1,2,0:T(8,128)}), f32[16,128,64]{1,2,0:T(8,128)S(1)}, u32[]{:S(2)}, u32[]{:S(2)}) %all-to-all-start.2) | async-done | bytes 524320 | tf_op jit(solution)/shard_map/all_to_all | solution.py:26
  97.2 6.1 %all-to-all-start.3 = ((f32[16,128,32]{1,2,0:T(8,128)}), f32[16,128,32]{1,2,0:T(8,128)S(1)}, u32[]{:S(2)}, u32[]{:S(2)}) async-start(f32[16,128,32]{1,2,0:T(8,128)} %bitcast.37), calls=%async_computation.3 | async-start | bytes 524288 | tf_op jit(solution)/shard_map/all_to_all | solution.py:26
  104.9 5.6 %all-to-all-done.3 = f32[16,128,32]{1,2,0:T(8,128)S(1)} async-done(((f32[16,128,32]{1,2,0:T(8,128)}), f32[16,128,32]{1,2,0:T(8,128)S(1)}, u32[]{:S(2)}, u32[]{:S(2)}) %all-to-all-start.3) | async-done | bytes 262176 | tf_op jit(solution)/shard_map/all_to_all | solution.py:26
  111.8 6.4 %all-to-all-start.4 = ((f32[16,128,16]{1,2,0:T(8,128)}), f32[16,128,16]{1,2,0:T(8,128)S(1)}, u32[]{:S(2)}, u32[]{:S(2)}) async-start(f32[16,128,16]{1,2,0:T(8,128)} %bitcast.45), calls=%async_computation.4 | async-start | bytes 262144 | tf_op jit(solution)/shard_map/all_to_all | solution.py:26
  119.3 6.5 %all-to-all-done.4 = f32[16,128,16]{1,2,0:T(8,128)S(1)} async-done(((f32[16,128,16]{1,2,0:T(8,128)}), f32[16,128,16]{1,2,0:T(8,128)S(1)}, u32[]{:S(2)}, u32[]{:S(2)}) %all-to-all-start.4) | async-done | bytes 131104 | tf_op jit(solution)/shard_map/all_to_all | solution.py:26
  127.9 4.0 %all-to-all-start.5 = ((f32[16,128,16]{1,2,0:T(8,128)}), f32[16,128,16]{1,2,0:T(8,128)S(1)}, u32[]{:S(2)}, u32[]{:S(2)}) async-start(f32[16,128,16]{1,2,0:T(8,128)} %bitcast.51), calls=%async_computation.5 | async-start | bytes 262144 | tf_op jit(solution)/shard_map/all_to_all | solution.py:26
  131.9 7.7 %all-to-all-done.5 = f32[16,128,16]{1,2,0:T(8,128)S(1)} async-done(((f32[16,128,16]{1,2,0:T(8,128)}), f32[16,128,16]{1,2,0:T(8,128)S(1)}, u32[]{:S(2)}, u32[]{:S(2)}) %all-to-all-start.5) | async-done | bytes 131104 | tf_op jit(solution)/shard_map/all_to_all | solution.py:26
  141.6 4.0 %all-to-all-start.6 = ((f32[16,128,32]{1,2,0:T(8,128)}), f32[16,128,32]{1,2,0:T(8,128)S(1)}, u32[]{:S(2)}, u32[]{:S(2)}) async-start(f32[16,128,32]{1,2,0:T(8,128)} %bitcast.56), calls=%async_computation.6 | async-start | bytes 524288 | tf_op jit(solution)/shard_map/all_to_all | solution.py:26
  148.1 4.2 %collective-permute-done.4 = f32[1,128,32]{2,1,0:T(8,128)S(1)} collective-permute-done((f32[1,128,32]{2,1,0:T(8,128)S(1)}, f32[1,128,32]{2,1,0:T(8,128)S(1)}, u32[]{:S(2)}, u32[]{:S(2)}) %collective-permute-start.4) | collective-permute-done | bytes 16416 | tf_op jit(solution)/shard_map/ppermute | solution.py:10
  155.6 7.6 %all-to-all-start.7 = ((f32[16,128,64]{1,2,0:T(8,128)}), f32[16,128,64]{1,2,0:T(8,128)S(1)}, u32[]{:S(2)}, u32[]{:S(2)}) async-start(f32[16,128,64]{1,2,0:T(8,128)} %bitcast.67), calls=%async_computation.7 | async-start | bytes 1048576 | tf_op jit(solution)/shard_map/all_to_all | solution.py:26
  163.1 5.3 %collective-permute-start.5 = (f32[2,128,64]{2,1,0:T(8,128)S(1)}, f32[2,128,64]{2,1,0:T(8,128)S(1)}, u32[]{:S(2)}, u32[]{:S(2)}) collective-permute-start(f32[2,128,64]{2,1,0:T(8,128)S(1)} %get-tuple-element.7), channel_id=1, source_target_pairs={{0,32},{8,40},{16,48},{24,56},{32,0},{40,8},{48,16},{56,24},{64,96... | collective-permute-start | bytes 196616 | tf_op jit(solution)/shard_map/ppermute | solution.py:10
  168.5 11.1 %collective-permute-done.5 = f32[2,128,64]{2,1,0:T(8,128)S(1)} collective-permute-done((f32[2,128,64]{2,1,0:T(8,128)S(1)}, f32[2,128,64]{2,1,0:T(8,128)S(1)}, u32[]{:S(2)}, u32[]{:S(2)}) %collective-permute-start.5) | collective-permute-done | bytes 65568 | tf_op jit(solution)/shard_map/ppermute | solution.py:10
  182.7 5.0 %all-to-all-start.8 = ((bf16[16,128,128]{2,1,0:T(8,128)(2,1)}), bf16[16,128,128]{2,1,0:T(8,128)(2,1)S(1)}, u32[]{:S(2)}, u32[]{:S(2)}) async-start(bf16[16,128,128]{2,1,0:T(8,128)(2,1)} %bitcast.76), calls=%async_computation.8 | async-start | bytes 1048576 | tf_op jit(solution)/shard_map/all_to_all | solution.py:26
  187.7 2.3 collective-permute-start.6
  190.6 16.0 %collective-permute-done.6 = bf16[3,128,128]{2,1,0:T(8,128)(2,1)S(1)} collective-permute-done((bf16[3,128,128]{2,1,0:T(8,128)(2,1)S(1)}, bf16[3,128,128]{2,1,0:T(8,128)(2,1)S(1)}, u32[]{:S(2)}, u32[]{:S(2)}) %collective-permute-start.6) | collective-permute-done | bytes 98336 | tf_op jit(solution)/shard_map/ppermute | solution.py:10
  210.8 4.9 %all-to-all-start.9 = ((bf16[16,128,256]{2,1,0:T(8,128)(2,1)}), bf16[16,128,256]{2,1,0:T(8,128)(2,1)S(1)}, u32[]{:S(2)}, u32[]{:S(2)}) async-start(bf16[16,128,256]{2,1,0:T(8,128)(2,1)} %bitcast.85), calls=%async_computation.9 | async-start | bytes 2097152 | tf_op jit(solution)/shard_map/all_to_all | solution.py:26
  217.2 17.8 %collective-permute-done.7 = bf16[4,128,256]{2,1,0:T(8,128)(2,1)S(1)} collective-permute-done((bf16[4,128,256]{2,1,0:T(8,128)(2,1)S(1)}, bf16[4,128,256]{2,1,0:T(8,128)(2,1)S(1)}, u32[]{:S(2)}, u32[]{:S(2)}) %collective-permute-start.7) | collective-permute-done | bytes 262176 | tf_op jit(solution)/shard_map/ppermute | solution.py:10
  (147 shorter events, 52.7 us)
Async XLA Ops:
  0.6 3.0 %copy-start = (bf16[1024,512]{1,0:T(8,128)(2,1)S(1)}, bf16[1024,512]{1,0:T(8,128)(2,1)}, u32[]{:S(2)}) copy-start(bf16[1024,512]{1,0:T(8,128)(2,1)} %param.6) | copy-start | bytes 3145732
  6.9 8.7 %copy-start.1 = (f32[5,128,512]{2,1,0:T(8,128)}, f32[5,128,512]{2,1,0:T(8,128)S(1)}, u32[]{:S(2)}) copy-start(f32[5,128,512]{2,1,0:T(8,128)S(1)} %convolution_subtract_fusion) | copy-start | bytes 3932164
  8.2 23.2 %all-to-all-start = ((bf16[16,128,256]{2,1,0:T(8,128)(2,1)}), bf16[16,128,256]{2,1,0:T(8,128)(2,1)S(1)}, u32[]{:S(2)}, u32[]{:S(2)}) async-start(bf16[16,128,256]{2,1,0:T(8,128)(2,1)} %bitcast.254), calls=%async_computation | async-start | bytes 2097152 | tf_op jit(solution)/shard_map/all_to_all | solution.py:26
  16.3 18.6 %collective-permute-start = (bf16[4,128,256]{2,1,0:T(8,128)(2,1)}, bf16[4,128,256]{2,1,0:T(8,128)(2,1)}, u32[]{:S(2)}, u32[]{:S(2)}) collective-permute-start(bf16[4,128,256]{2,1,0:T(8,128)(2,1)} %select_convert_fusion), channel_id=1, source_target_pairs={{0,8},{8,0},{16,24},{24,16},{32,40},{40,32},{48,56},{56,48},{64,72... | collective-permute-start | bytes 786440 | tf_op jit(solution)/shard_map/ppermute | solution.py:10
  37.0 27.0 %all-to-all-start.1 = ((bf16[16,128,128]{2,1,0:T(8,128)(2,1)}), bf16[16,128,128]{2,1,0:T(8,128)(2,1)}, u32[]{:S(2)}, u32[]{:S(2)}) async-start(bf16[16,128,128]{2,1,0:T(8,128)(2,1)} %bitcast.20), calls=%async_computation.1 | async-start | bytes 1048576 | tf_op jit(solution)/shard_map/all_to_all | solution.py:26
  45.5 19.8 %slice-start.1 = ((bf16[1,15,128,1024]{3,2,1,0:T(8,128)(2,1)}), bf16[1,4,128,1024]{3,2,1,0:T(8,128)(2,1)S(1)}, s32[]{:S(2)}) async-start(bf16[1,15,128,1024]{3,2,1,0:T(8,128)(2,1)} %param.11), calls=%async_computation.11 | async-start | bytes 2097152 | tf_op jit(solution)/shard_map/slice | solution.py:92
  45.5 20.2 %collective-permute-start.1 = (bf16[3,128,128]{2,1,0:T(8,128)(2,1)}, bf16[3,128,128]{2,1,0:T(8,128)(2,1)}, u32[]{:S(2)}, u32[]{:S(2)}) collective-permute-start(bf16[3,128,128]{2,1,0:T(8,128)(2,1)} %select_convert_fusion.1), channel_id=1, source_target_pairs={{0,16},{8,24},{16,0},{24,8},{32,48},{40,56},{48,32},{56,40},{64,80... | collective-permute-start | bytes 294920 | tf_op jit(solution)/shard_map/ppermute | solution.py:10
  67.7 26.5 %slice-start.2 = ((bf16[1,15,128,1024]{3,2,1,0:T(8,128)(2,1)}), bf16[1,3,128,1024]{3,2,1,0:T(8,128)(2,1)S(1)}, s32[]{:S(2)}) async-start(bf16[1,15,128,1024]{3,2,1,0:T(8,128)(2,1)} %param.11), calls=%async_computation.12 | async-start | bytes 1572864 | tf_op jit(solution)/shard_map/slice | solution.py:92
  67.7 26.5 %all-to-all-start.2 = ((f32[16,128,64]{1,2,0:T(8,128)}), f32[16,128,64]{1,2,0:T(8,128)S(1)}, u32[]{:S(2)}, u32[]{:S(2)}) async-start(f32[16,128,64]{1,2,0:T(8,128)} %bitcast.29), calls=%async_computation.2 | async-start | bytes 1048576 | tf_op jit(solution)/shard_map/all_to_all | solution.py:26
  75.7 19.5 %collective-permute-start.2 = (f32[2,128,64]{2,1,0:T(8,128)}, f32[2,128,64]{2,1,0:T(8,128)}, u32[]{:S(2)}, u32[]{:S(2)}) collective-permute-start(f32[2,128,64]{2,1,0:T(8,128)} %slice_select_fusion), channel_id=1, source_target_pairs={{0,32},{8,40},{16,48},{24,56},{32,0},{40,8},{48,16},{56,24},{64,96... | collective-permute-start | bytes 196616 | tf_op jit(solution)/shard_map/ppermute | solution.py:10
  96.2 14.3 %slice-start.3 = ((bf16[1,15,128,1024]{3,2,1,0:T(8,128)(2,1)}), bf16[1,2,128,1024]{3,2,1,0:T(8,128)(2,1)S(1)}, s32[]{:S(2)}) async-start(bf16[1,15,128,1024]{3,2,1,0:T(8,128)(2,1)} %param.11), calls=%async_computation.13 | async-start | bytes 1048576 | tf_op jit(solution)/shard_map/slice | solution.py:92
  97.2 13.3 %all-to-all-start.3 = ((f32[16,128,32]{1,2,0:T(8,128)}), f32[16,128,32]{1,2,0:T(8,128)S(1)}, u32[]{:S(2)}, u32[]{:S(2)}) async-start(f32[16,128,32]{1,2,0:T(8,128)} %bitcast.37), calls=%async_computation.3 | async-start | bytes 524288 | tf_op jit(solution)/shard_map/all_to_all | solution.py:26
  103.4 7.4 %collective-permute-start.3 = (f32[1,128,32]{2,1,0:T(8,128)S(1)}, f32[1,128,32]{2,1,0:T(8,128)S(1)}, u32[]{:S(2)}, u32[]{:S(2)}) collective-permute-start(f32[1,128,32]{2,1,0:T(8,128)S(1)} %slice_select_fusion.1), channel_id=1, source_target_pairs={{0,64},{8,72},{16,80},{24,88},{32,96},{40,104},{48,112},{56,120},{... | collective-permute-start | bytes 49160 | tf_op jit(solution)/shard_map/ppermute | solution.py:10
  111.8 14.0 %all-to-all-start.4 = ((f32[16,128,16]{1,2,0:T(8,128)}), f32[16,128,16]{1,2,0:T(8,128)S(1)}, u32[]{:S(2)}, u32[]{:S(2)}) async-start(f32[16,128,16]{1,2,0:T(8,128)} %bitcast.45), calls=%async_computation.4 | async-start | bytes 262144 | tf_op jit(solution)/shard_map/all_to_all | solution.py:26
  127.9 11.7 %all-to-all-start.5 = ((f32[16,128,16]{1,2,0:T(8,128)}), f32[16,128,16]{1,2,0:T(8,128)S(1)}, u32[]{:S(2)}, u32[]{:S(2)}) async-start(f32[16,128,16]{1,2,0:T(8,128)} %bitcast.51), calls=%async_computation.5 | async-start | bytes 262144 | tf_op jit(solution)/shard_map/all_to_all | solution.py:26
  141.6 11.2 %all-to-all-start.6 = ((f32[16,128,32]{1,2,0:T(8,128)}), f32[16,128,32]{1,2,0:T(8,128)S(1)}, u32[]{:S(2)}, u32[]{:S(2)}) async-start(f32[16,128,32]{1,2,0:T(8,128)} %bitcast.56), calls=%async_computation.6 | async-start | bytes 524288 | tf_op jit(solution)/shard_map/all_to_all | solution.py:26
  145.7 6.5 %collective-permute-start.4 = (f32[1,128,32]{2,1,0:T(8,128)S(1)}, f32[1,128,32]{2,1,0:T(8,128)S(1)}, u32[]{:S(2)}, u32[]{:S(2)}) collective-permute-start(f32[1,128,32]{2,1,0:T(8,128)S(1)} %bitcast.271), channel_id=1, source_target_pairs={{0,64},{8,72},{16,80},{24,88},{32,96},{40,104},{48,112},{56,120},{... | collective-permute-start | bytes 49160 | tf_op jit(solution)/shard_map/ppermute | solution.py:10
  155.6 24.0 %all-to-all-start.7 = ((f32[16,128,64]{1,2,0:T(8,128)}), f32[16,128,64]{1,2,0:T(8,128)S(1)}, u32[]{:S(2)}, u32[]{:S(2)}) async-start(f32[16,128,64]{1,2,0:T(8,128)} %bitcast.67), calls=%async_computation.7 | async-start | bytes 1048576 | tf_op jit(solution)/shard_map/all_to_all | solution.py:26
  163.1 16.4 %collective-permute-start.5 = (f32[2,128,64]{2,1,0:T(8,128)S(1)}, f32[2,128,64]{2,1,0:T(8,128)S(1)}, u32[]{:S(2)}, u32[]{:S(2)}) collective-permute-start(f32[2,128,64]{2,1,0:T(8,128)S(1)} %get-tuple-element.7), channel_id=1, source_target_pairs={{0,32},{8,40},{16,48},{24,56},{32,0},{40,8},{48,16},{56,24},{64,96... | collective-permute-start | bytes 196616 | tf_op jit(solution)/shard_map/ppermute | solution.py:10
  182.7 24.0 %all-to-all-start.8 = ((bf16[16,128,128]{2,1,0:T(8,128)(2,1)}), bf16[16,128,128]{2,1,0:T(8,128)(2,1)S(1)}, u32[]{:S(2)}, u32[]{:S(2)}) async-start(bf16[16,128,128]{2,1,0:T(8,128)(2,1)} %bitcast.76), calls=%async_computation.8 | async-start | bytes 1048576 | tf_op jit(solution)/shard_map/all_to_all | solution.py:26
  187.7 18.9 %collective-permute-start.6 = (bf16[3,128,128]{2,1,0:T(8,128)(2,1)S(1)}, bf16[3,128,128]{2,1,0:T(8,128)(2,1)S(1)}, u32[]{:S(2)}, u32[]{:S(2)}) collective-permute-start(bf16[3,128,128]{2,1,0:T(8,128)(2,1)S(1)} %get-tuple-element.5), channel_id=1, source_target_pairs={{0,16},{8,24},{16,0},{24,8},{32,48},{40,56},{48,32},{56,40},{64,80... | collective-permute-start | bytes 294920 | tf_op jit(solution)/shard_map/ppermute | solution.py:10
  210.8 25.2 %all-to-all-start.9 = ((bf16[16,128,256]{2,1,0:T(8,128)(2,1)}), bf16[16,128,256]{2,1,0:T(8,128)(2,1)S(1)}, u32[]{:S(2)}, u32[]{:S(2)}) async-start(bf16[16,128,256]{2,1,0:T(8,128)(2,1)} %bitcast.85), calls=%async_computation.9 | async-start | bytes 2097152 | tf_op jit(solution)/shard_map/all_to_all | solution.py:26
  215.7 19.3 %collective-permute-start.7 = (bf16[4,128,256]{2,1,0:T(8,128)(2,1)S(1)}, bf16[4,128,256]{2,1,0:T(8,128)(2,1)S(1)}, u32[]{:S(2)}, u32[]{:S(2)}) collective-permute-start(bf16[4,128,256]{2,1,0:T(8,128)(2,1)S(1)} %get-tuple-element.3), channel_id=1, source_target_pairs={{0,8},{8,0},{16,24},{24,16},{32,40},{40,32},{48,56},{56,48},{64,72... | collective-permute-start | bytes 786440 | tf_op jit(solution)/shard_map/ppermute | solution.py:10
  236.2 2.4 %copy-start.3 = (f32[8,128,512]{2,1,0:T(8,128)S(1)}, f32[8,128,512]{2,1,0:T(8,128)}, u32[]{:S(2)}) copy-start(f32[8,128,512]{2,1,0:T(8,128)} %get-tuple-element.39) | copy-start | bytes 6291460
  (9 other events, 11.8 us)

commit v2 on v0

v2 whole, which is shorter than its diff:
```python
import functools

import jax
import jax.numpy as jnp
from jax import lax
from jax.experimental import pallas as pl
from jax.experimental.pallas import tpu as pltpu
from jax.sharding import PartitionSpec as P

BF = jnp.bfloat16
F32 = jnp.float32
LEVELS = 5
SEP = 128
COLS = 128
CHIPS = 4
AXES = ("layer", "row")
VMEM = pl.BlockSpec(memory_space=pltpu.VMEM)
SMEM = pl.BlockSpec(memory_space=pltpu.SMEM)
ANY = pl.BlockSpec(memory_space=pl.ANY)
PARAMS = pltpu.CompilerParams(vmem_limit_bytes=16 * 1024 * 1024)


def block_start(level):
    return level * LEVELS - level * (level - 1) // 2


def devices():
    return lax.axis_size("layer") * lax.axis_size("row")


def send_xor(value, mask):
    return lax.ppermute(value, AXES, [(i, i ^ mask) for i in range(devices())])


def send_ring(value, step):
    pairs = [(i, (i & ~6) | ((((i >> 1 & 3) + step) % CHIPS) << 1)) for i in range(devices())]
    return lax.ppermute(value, AXES, pairs)


def lanes(start, size=128):
    return pl.ds(pl.multiple_of(start * size, size), size)


def dot(a, b):
    return jnp.dot(a, b, preferred_element_type=F32)


def masked_into(cm, coup, pattern, t):
    for k in range(8):
        rows = pl.ds(k * 128, 128)
        keep = pattern[k, t].astype(F32)
        cm[rows, :] = (coup[t, rows, :].astype(F32) * keep).astype(BF)


def leaf_kernel(pos, pattern, rhs, inv, coup, anc, own0, s1, s2, s3, own, side, cross, share, yb, cm):
    for k in range(8):
        rows = pl.ds(k * 128, 128)
        yb[rows, :] = dot(inv[k], rhs[rows, :]).astype(BF)
    group = pos[2]
    for t in range(LEVELS):
        masked_into(cm, coup, pattern, t)
        terms = lax.dot_general(cm[...], yb[...], (((0,), (0,)), ((), ())), preferred_element_type=F32)
        share[...] = anc[t] - terms
        mine = share[:, lanes(group)]
        others = [share[:, lanes(group ^ m)].astype(BF) for m in (1, 2, 3)]
        if t == 0:
            own0[...] = mine
            for out, piece in zip((s1, s2, s3), others):
                out[...] = piece
        else:
            own[t - 1] = mine
            cross[t - 1, 0] = others[0]
            side[t - 1] = others[1]
            cross[t - 1, 1] = others[2]


def rows_of(blocks, first, count):
    return blocks[first : first + count].reshape(count * SEP, 1024)


def fetch(own_blocks, oth_blocks, runs, blk, fulls, sems):
    copies, at = [], 0
    for first, count in runs:
        for side, blocks in enumerate((own_blocks, oth_blocks)):
            source, target = blocks.at[pl.ds(first, count)], blk.at[side, pl.ds(at, count)]
            copies.append(pltpu.make_async_copy(source, target, sems.at[len(copies)]))
        at += count
    for source, target in fulls:
        copies.append(pltpu.make_async_copy(source, target, sems.at[len(copies)]))
    for one in copies:
        one.start()
    return copies


def wait(copies):
    for one in copies:
        one.wait()


def forward_kernel(level, pos, own_blocks, oth_blocks, z0, z1, z2, z3, *refs):
    count = LEVELS - level
    first = block_start(level)
    if level == 0:
        own, got_core, got_layer, y_out, pend_out, v_out, zabs, blk, sems = refs
    else:
        pend, y_out, pend_out, v_out, zabs, blk, sems = refs
    copies = fetch(own_blocks, oth_blocks, [(first, count)], blk, [], sems)
    chip, core = pos[0], pos[1]
    for d, z in enumerate((z0, z1, z2, z3)):
        zabs[lanes((chip + CHIPS - d) % CHIPS, 256), :] = z[...]
    for side, half in enumerate((core, 1 - core)):
        copies[side].wait()
        product = dot(rows_of(blk.at[side], 0, count), zabs[...])
        y_out[:, lanes(half)] = product[:SEP].T.astype(BF)
        for k in range(count - 1):
            if level == 0:
                base = own[k] if side == 0 else got_core[k, 0].astype(F32)
                base = base + got_layer[k, side].astype(F32)
            else:
                base = pend[k + 1, lanes(half), :]
            after = base - product[(k + 1) * SEP : (k + 2) * SEP]
            pend_out[k, lanes(half), :] = after
            if level == 0 and k == 0:
                v_out[lanes(half), :] = after.astype(BF)
            if level == 1 and k < 2:
                v_out[k, lanes(half), :] = after.astype(BF)


def middle_kernel(pos, own_blocks, oth_blocks, full, z0, z1, z2, z3, pend, y2, y3, v_out, zabs, vabs, blk, whole, sems):
    copies = fetch(own_blocks, oth_blocks, [(9, 1), (11, 3)], blk, [(full, whole)], sems)
    chip, core = pos[0], pos[1]
    for d, z in enumerate((z0, z1, z2, z3)):
        place = lanes((chip + CHIPS - d) % CHIPS, 256)
        zabs[place, :] = z[0]
        vabs[place, :] = z[1]
    copies[4].wait()
    vabs[...] = (vabs[...].astype(F32) - dot(whole[...], zabs[...])).astype(BF)
    wait(copies[:4])
    for side, half in enumerate((core, 1 - core)):
        two = dot(rows_of(blk.at[side], 0, 2), zabs[...])
        three = dot(rows_of(blk.at[side], 2, 2), vabs[...])
        y2[:, lanes(half)] = two[:SEP].T.astype(BF)
        y3[:, lanes(half)] = three[:SEP].T.astype(BF)
        after = pend[2, lanes(half), :] - two[SEP:] - three[SEP:]
        v_out[lanes(half), :] = after.astype(BF)


def hand_out(part, level_at, chip, outs):
    for d, out in enumerate(outs):
        out[level_at] = part[:, lanes((chip + d) % CHIPS, 256)].astype(out.dtype)


def top_kernel(pos, own_blocks, oth_blocks, full3, full4, z0, z1, z2, z3, y2, y3, sol_out, solb_out, *refs):
    outs, (zabs, part, blk, whole3, whole4, sems) = refs[:4], refs[4:]
    copies = fetch(own_blocks, oth_blocks, [(9, 1), (11, 3)], blk, [(full4, whole4), (full3, whole3)], sems)
    chip, core = pos[0], pos[1]
    for d, z in enumerate((z0, z1, z2, z3)):
        zabs[lanes((chip + CHIPS - d) % CHIPS, 256), :] = z[...]
    copies[4].wait()
    y4 = dot(whole4[...], zabs[...]).T.astype(BF)
    sol = dot(y4, whole4[:, lanes(chip, 256)])
    sol_out[...] = sol
    solb_out[...] = sol.astype(BF)
    third = second = None
    wait(copies[:4])
    for side, half in enumerate((core, 1 - core)):
        minus = -solb_out[:, lanes(half)]
        one = dot(jnp.concatenate([y3[:, lanes(half)], minus], axis=1), rows_of(blk.at[side], 2, 2))
        two = dot(jnp.concatenate([y2[:, lanes(half)], minus], axis=1), rows_of(blk.at[side], 0, 2))
        third = one if third is None else third + one
        second = two if second is None else second + two
    part[...] = third
    hand_out(part, 1, chip, outs)
    copies[5].wait()
    part[...] = second - dot(third.astype(BF), whole3[...])
    hand_out(part, 0, chip, outs)


def low_kernel(pos, own_blocks, oth_blocks, full1, held, g1, g2, g3, sol4, y0, y1, sol_out, solb_out, *refs):
    outs, (part, vals, blk, whole1, sems) = refs[:4], refs[4:]
    copies = fetch(own_blocks, oth_blocks, [(0, 1), (2, 7)], blk, [(full1, whole1)], sems)
    chip, core = pos[0], pos[1]
    for k in range(2):
        sol = held[k] + g1[k].astype(F32) + g2[k].astype(F32) + g3[k].astype(F32)
        sol_out[k] = sol
        solb_out[k] = sol.astype(BF)
    solb_out[2] = sol4[...]
    first = zeroth = None
    wait(copies[:4])
    for side, half in enumerate((core, 1 - core)):
        vals[:, 0:SEP] = y1[:, lanes(half)]
        for k in range(3):
            vals[:, SEP * (k + 1) : SEP * (k + 2)] = -solb_out[k, :, lanes(half)]
        one = dot(vals[...], rows_of(blk.at[side], 4, 4))
        both = jnp.concatenate([y0[:, lanes(half)], vals[:, SEP:]], axis=1)
        two = dot(both, rows_of(blk.at[side], 0, 4))
        first = one if first is None else first + one
        zeroth = two if zeroth is None else zeroth + two
    part[...] = first
    hand_out(part, 1, chip, outs)
    copies[4].wait()
    part[...] = zeroth - dot(first.astype(BF), whole1[...])
    hand_out(part, 0, chip, outs)


def final_kernel(pos, pattern, rhs, inv, coup, sol01, got1, got2, got3, sol23, sol4, layer_b, core_b, x_leaf, x_anc, solved, cm, back):
    group, core = pos[2], pos[1]
    mine = lanes(core)
    for t in range(LEVELS):
        if t < 2:
            own = sol01[t, :, mine]
            others = got1[t], got2[t], got3[t]
        else:
            own = sol23[t - 2, :, mine] if t < 4 else sol4[:, mine]
            others = core_b[t - 2, 0], layer_b[t - 2, :, mine], core_b[t - 2, 1]
        x_anc[t, :, lanes(group)] = own.T
        for m in range(1, 4):
            x_anc[t, :, lanes(group ^ m)] = others[m - 1].astype(F32).T
        solved[...] = x_anc[t].astype(BF)
        masked_into(cm, coup, pattern, t)
        terms = dot(cm[...], solved[...])
        if t == 0:
            back[...] = terms
        else:
            back[...] += terms
    for k in range(8):
        rows = pl.ds(k * 128, 128)
        leaf_vb = (dot(inv[k], rhs[rows, :]) - back[rows, :]).astype(BF)
        x_leaf[rows, :] = lax.dot_general(inv[k], leaf_vb, (((0,), (0,)), ((), ())), preferred_element_type=F32)


def shape(dims, dtype):
    return jax.ShapeDtypeStruct(dims, dtype)


def call(kernel, name, outs, scratch, copies, *args):
    specs = [SMEM if a.dtype == jnp.int32 else ANY if copies and a.shape[-1] == 1024 else VMEM for a in args]
    scratch = [pltpu.VMEM(dims, dtype) for dims, dtype in scratch]
    return pl.pallas_call(
        kernel,
        out_shape=outs,
        in_specs=specs,
        out_specs=[VMEM] * len(outs),
        scratch_shapes=scratch + ([pltpu.SemaphoreType.DMA((copies,))] if copies else []),
        compiler_params=PARAMS,
        name=name,
    )(*args)


def add(*values):
    return functools.reduce(jnp.add, [v.astype(F32) for v in values]).astype(BF)


def ring(value):
    return [value] + [send_ring(value, d) for d in (1, 2, 3)]


def body(leaf_rhs, leaf_inv, coupling, pattern, anc_rhs, anc_blocks):
    layer, row = lax.axis_index("layer"), lax.axis_index("row")
    chip, core = row // 2, row % 2
    group = (layer % 2) * 2 + core
    flip = core == 1
    pos = jnp.stack([chip, core, group]).astype(jnp.int32)
    coup = coupling.transpose(1, 0, 2)
    blocks = anc_blocks[0]

    def whole(k):
        return lax.all_gather(blocks[k], "row", axis=0, tiled=True)

    full3, full4, full1 = whole(10), whole(14), whole(1)

    own0, s1, s2, s3, own, side, cross = call(
        leaf_kernel,
        "leaf_forward",
        [shape((SEP, COLS), F32)]
        + [shape((SEP, COLS), BF)] * 3
        + [shape((4, SEP, COLS), F32), shape((4, SEP, COLS), BF), shape((4, 2, SEP, COLS), BF)],
        [((SEP, 512), F32), ((1024, 512), BF), ((1024, 128), BF)],
        0,
        *(pos, pattern, leaf_rhs, leaf_inv, coup, anc_rhs[0]),
    )
    late_blocks, s1 = lax.optimization_barrier((blocks, s1))
    got = [send_xor(s, m) for s, m in zip((s1, s2, s3), (1, 8, 9))]
    got_core = send_xor(cross, 1)
    oth = send_xor(late_blocks, 1)
    got_layer = send_xor(jnp.stack([side, got_core[:, 1]], axis=1), 8)
    near = own0 + got[1].astype(F32)
    far = got[0].astype(F32) + got[2].astype(F32)
    v = jnp.concatenate([jnp.where(flip, far, near), jnp.where(flip, near, far)]).astype(BF)

    zscratch, wide = ((1024, COLS), BF), ((1024, 1024), BF)
    y0, pend, v = call(
        functools.partial(forward_kernel, 0),
        "forward_level0",
        [shape((COLS, 256), BF), shape((4, 256, COLS), F32), shape((256, COLS), BF)],
        [zscratch, ((2, 5, SEP, 1024), BF)],
        2,
        *(pos, blocks, oth, *ring(v), own, got_core, got_layer),
    )
    y1, pend, v = call(
        functools.partial(forward_kernel, 1),
        "forward_level1",
        [shape((COLS, 256), BF), shape((3, 256, COLS), F32), shape((2, 256, COLS), BF)],
        [zscratch, ((2, 4, SEP, 1024), BF)],
        2,
        *(pos, blocks, oth, *ring(v), pend),
    )
    y2, y3, v = call(
        middle_kernel,
        "forward_levels23",
        [shape((COLS, 256), BF), shape((COLS, 256), BF), shape((256, COLS), BF)],
        [zscratch, zscratch, ((2, 4, SEP, 1024), BF), wide],
        5,
        *(pos, blocks, oth, full3, *ring(v), pend),
    )
    v = add(v, *[send_xor(v, m) for m in (16, 32, 48)])
    v, y1, y2, y3 = lax.optimization_barrier((v, y1, y2, y3))
    z4 = add(v, *[send_xor(v, m) for m in (64, 128, 192)])
    low = jnp.stack([y2, y3])
    low = add(low, *[send_xor(low, m) for m in (16, 32, 48)])
    y3 = add(low[1], send_xor(low[1], 64))
    y2 = low[0]
    y1 = add(y1, send_xor(y1, 16))
    pieces = [shape((2, COLS, 256), F32)] + [shape((2, COLS, 256), BF)] * 3
    sol4, sol4b, *parts = call(
        top_kernel,
        "top_levels",
        [shape((COLS, 256), F32), shape((COLS, 256), BF)] + pieces,
        [zscratch, ((COLS, 1024), F32), ((2, 4, SEP, 1024), BF), wide, wide],
        6,
        *(pos, blocks, oth, full3, full4, *ring(z4), y2, y3),
    )
    parts = [parts[0]] + [send_ring(parts[d], d) for d in (1, 2, 3)]
    sol23, upper, *parts = call(
        low_kernel,
        "low_levels",
        [shape((2, COLS, 256), F32), shape((3, COLS, 256), BF)] + pieces,
        [((COLS, 1024), F32), ((COLS, 4 * SEP), BF), ((2, 8, SEP, 1024), BF), wide],
        5,
        *(pos, blocks, oth, full1, *parts, sol4b, y0, y1),
    )
    parts = [parts[0]] + [send_ring(parts[d], d) for d in (1, 2, 3)]

    def halves(value):
        low, high = value[..., :SEP], value[..., SEP:]
        return jnp.where(flip, high, low), jnp.where(flip, low, high)

    layer_b = send_xor(upper, 8)
    core_b = send_xor(jnp.stack([halves(upper)[1], halves(layer_b)[1]], axis=1), 1)
    sol01 = parts[0] + parts[1].astype(F32) + parts[2].astype(F32) + parts[3].astype(F32)
    same, other = halves(sol01.astype(BF))
    got = [send_xor(other, 1), send_xor(same, 8), send_xor(other, 9)]
    x_leaf, x_anc = call(
        final_kernel,
        "leaf_backward",
        [shape((1024, 512), F32), shape((LEVELS, SEP, 512), F32)],
        [((SEP, 512), BF), ((1024, 128), BF), ((1024, 512), F32)],
        0,
        *(pos, pattern, leaf_rhs, leaf_inv, coup, sol01, *got, sol23, sol4, layer_b, core_b),
    )
    return x_leaf, x_anc[None]


def solution(mesh):
    placed = (
        P(("layer", "row"), None),
        P(("layer", "row"), None, None),
        P(("layer", "row"), None, None),
        P(("layer", "row"), None),
        P("layer", None, "row", None),
        P("layer", None, "row", None),
    )
    return jax.shard_map(
        body,
        mesh=mesh,
        in_specs=placed,
        out_specs=(P(("layer", "row"), None), P("layer", None, "row", None)),
        check_vma=False,
    )
```

time: 552 us -> 170 us (0.31)
  waiting for transfers between devices: 421 us -> 40.7 us
  matrix products: 30.4 us -> 0 us
  Pallas kernels: 0 us -> 26.8 us
  starting transfers between devices: 42.9 us -> 64.7 us
  other arithmetic: 13.9 us -> 1.34 us
    reduce_scatter x5 -> x0, waiting for transfers between devices: 169 us -> none  [body(): lax.psum_scatter(transposed(jnp.int32(0), sep_rows * lax.axis_size('row')...]
    all_gather x5 -> x3, waiting for transfers between devices: 134 us -> 0.04 us  [whole(): return lax.all_gather(blocks[k], 'row', axis=0, tiled=True)]
    ppermute x15 -> x40, waiting for transfers between devices: 117 us -> 39.9 us  [the longest x18 22.6 us: send_ring(): return lax.ppermute(value, AXES, pairs)]
    dot_general x13 -> x0, matrix products: 30.4 us -> none  [the longest x5 17.2 us: transposed(): lax.dot_general(factor, stacked_vals, (((0, 1), (0, 1)), ((), ())), prefe...]
    pallas_call x0 -> x7, Pallas kernels: none -> 26.8 us  [call(): pl.pallas_call(kernel, out_shape=outs, in_specs=specs, out_specs=[VMEM] *...]
    ppermute x15 -> x40, starting transfers between devices: 42.4 us -> 64.6 us  [the longest x22 41.9 us: send_xor(): return lax.ppermute(value, AXES, [(i, i ^ mask) for i in range(devices())])]
    slice x4 -> x2, local copies, waits for them, and re-layouts: 8.73 us -> 2.12 us  [the longest x1 2.11 us: whole(): return lax.all_gather(blocks[k], 'row', axis=0, tiled=True)]
    unnamed x48 -> x56, local copies, waits for them, and re-layouts: 14.3 us -> 19.3 us
  transfers between devices with their start and end apart: 25 -> 43, of which waited for: 25 -> 22; matrix products, arithmetic and copies ran while one was open for 2% -> 1% of each run, Pallas kernels for 0% -> 10%
where the time goes in v2:
time: 170 us
  starting transfers between devices  64.7 us (38%)
  waiting for transfers between devices  40.7 us (24%)
  Pallas kernels  26.8 us (16%)
  local copies, waits for them, and re-layouts  22.1 us (13%)
  between operations  14.1 us (8%)
    ppermute x22, starting transfers between devices, send_xor(): return lax.ppermute(value, AXES, [(i, i ^ mask) for i in range(devices())])  41.9 us
    pallas_call x7, Pallas kernels, call(): pl.pallas_call(kernel, out_shape=outs, in_specs=specs, out_specs=[VMEM] *...  26.8 us
    ppermute x18, starting transfers between devices, send_ring(): return lax.ppermute(value, AXES, pairs)  22.7 us
    ppermute x18, waiting for transfers between devices, send_ring(): return lax.ppermute(value, AXES, pairs)  22.6 us
    unnamed x56, local copies, waits for them, and re-layouts  19.3 us
    ppermute x22, waiting for transfers between devices, send_xor(): return lax.ppermute(value, AXES, [(i, i ^ mask) for i in range(devices())])  17.3 us
  transfers between devices with their start and end apart: 43, of which 22 were waited for; matrix products, arithmetic and copies ran while one was open for 1% of the time, Pallas kernels for 10%

profile of v2, /device:TPU:1, one launch (start us, length us, event | category | flops | bytes accessed | tf_op | source)
XLA Modules:
  0.0 169.7 jit_solution(11808671154221244792)
XLA Ops:
  14.8 3.3 %collective-permute-start = (bf16[15,128,1024]{2,1,0:T(8,128)(2,1)}, bf16[15,128,1024]{2,1,0:T(8,128)(2,1)}, u32[]{:S(2)}, u32[]{:S(2)}) collective-permute-start(bf16[15,128,1024]{2,1,0:T(8,128)(2,1)} %bitcast.4.own_blocks), channel_id=1, source_target_pairs={{0,1},{1,0},{2,3},{3,2},{4,5},{5,4},{6,7},{7,6},{8,9},{9,8},{10,11... | collective-permute-start | bytes 11796488 | tf_op jit(solution)/shard_map/ppermute | solution.py:32
  20.2 4.6 %collective-permute-done.7.refs_1_ = bf16[4,2,128,128]{3,2,1,0:T(8,128)(2,1)S(1)} collective-permute-done((bf16[4,2,128,128]{3,2,1,0:T(8,128)(2,1)S(1)}, bf16[4,2,128,128]{3,2,1,0:T(8,128)(2,1)S(1)}, u32[]{:S(2)}, u32[]{:S(2)}) %collective-permute-start.7) | collective-permute-done | bytes 262176 | tf_op jit(solution)/shard_map/ppermute | solution.py:32
  26.2 2.6 %collective-permute-start.5 = (bf16[256,128]{1,0:T(8,128)(2,1)S(1)}, bf16[256,128]{1,0:T(8,128)(2,1)S(1)}, u32[]{:S(2)}, u32[]{:S(2)}) collective-permute-start(bf16[256,128]{1,0:T(8,128)(2,1)S(1)} %pad_maximum_fusion.3.z0), channel_id=1, source_target_pairs={{0,4},{1,5},{2,6},{3,7},{4,0},{5,1},{6,2},{7,3},{8,12},{9,13},{10,... | collective-permute-start | bytes 196616 | tf_op jit(solution)/shard_map/ppermute | solution.py:37
  29.9 5.2 %collective-permute-done.5.z2 = bf16[256,128]{1,0:T(8,128)(2,1)S(1)} collective-permute-done((bf16[256,128]{1,0:T(8,128)(2,1)S(1)}, bf16[256,128]{1,0:T(8,128)(2,1)S(1)}, u32[]{:S(2)}, u32[]{:S(2)}) %collective-permute-start.5) | collective-permute-done | bytes 65568 | tf_op jit(solution)/shard_map/ppermute | solution.py:37
  35.2 3.5 %forward_level0.1 = (bf16[128,256]{1,0:T(8,128)(2,1)S(1)}, f32[4,256,128]{2,1,0:T(8,128)S(1)}, bf16[256,128]{1,0:T(8,128)(2,1)S(1)}) custom-call(s32[3]{0:T(128)S(1)} %pad_add_fusion.pos, bf16[15,128,1024]{2,1,0:T(8,128)(2,1)} %bitcast.4.own_blocks, bf16[15,128,1024]{2,1,0:T(8,128)(2,1)} %collective-permute-done.oth_blocks, ...), custom_call_target="tpu_custom_call" | custom-call | tf_op jit(solution)/shard_map/forward_level0/pallas_call | solution.py:239
  45.9 3.7 %forward_level1.1 = (bf16[128,256]{1,0:T(8,128)(2,1)}, f32[3,256,128]{2,1,0:T(8,128)S(1)}, bf16[2,256,128]{2,1,0:T(8,128)(2,1)S(1)}) custom-call(s32[3]{0:T(128)S(1)} %pad_add_fusion.pos, bf16[15,128,1024]{2,1,0:T(8,128)(2,1)} %bitcast.4.own_blocks, bf16[15,128,1024]{2,1,0:T(8,128)(2,1)} %collective-permute-done.oth_blocks, ...), custom_call_target="tpu_custom_call" | custom-call | tf_op jit(solution)/shard_map/forward_level1/pallas_call | solution.py:239
  53.2 3.7 %collective-permute-done.12.z1 = bf16[2,256,128]{2,1,0:T(8,128)(2,1)S(1)} collective-permute-done((bf16[2,256,128]{2,1,0:T(8,128)(2,1)S(1)}, bf16[2,256,128]{2,1,0:T(8,128)(2,1)S(1)}, u32[]{:S(2)}, u32[]{:S(2)}) %collective-permute-start.12) | collective-permute-done | bytes 131104 | tf_op jit(solution)/shard_map/ppermute | solution.py:37
  64.2 3.5 %forward_levels23.1 = (bf16[128,256]{1,0:T(8,128)(2,1)S(1)}, bf16[128,256]{1,0:T(8,128)(2,1)S(1)}, bf16[256,128]{1,0:T(8,128)(2,1)S(1)}) custom-call(s32[3]{0:T(128)S(1)} %pad_add_fusion.pos, bf16[15,128,1024]{2,1,0:T(8,128)(2,1)} %bitcast.4.own_blocks, bf16[15,128,1024]{2,1,0:T(8,128)(2,1)} %collective-permute-done.oth_blocks, ...), custom_call_target="tpu_custom_call" | custom-call | tf_op jit(solution)/shard_map/forward_levels23/pallas_call | solution.py:239
  67.8 3.1 %collective-permute-start.15 = (bf16[256,128]{1,0:T(8,128)(2,1)S(1)}, bf16[256,128]{1,0:T(8,128)(2,1)S(1)}, u32[]{:S(2)}, u32[]{:S(2)}) collective-permute-start(bf16[256,128]{1,0:T(8,128)(2,1)S(1)} %get-tuple-element.51), channel_id=1, source_target_pairs={{0,16},{1,17},{2,18},{3,19},{4,20},{5,21},{6,22},{7,23},{8,24},{9,... | collective-permute-start | bytes 196616 | tf_op jit(solution)/shard_map/ppermute | solution.py:32
  70.9 4.4 %collective-permute-start.16 = (bf16[256,128]{1,0:T(8,128)(2,1)S(1)}, bf16[256,128]{1,0:T(8,128)(2,1)S(1)}, u32[]{:S(2)}, u32[]{:S(2)}) collective-permute-start(bf16[256,128]{1,0:T(8,128)(2,1)S(1)} %get-tuple-element.51), channel_id=1, source_target_pairs={{0,32},{1,33},{2,34},{3,35},{4,36},{5,37},{6,38},{7,39},{8,40},{9,... | collective-permute-start | bytes 196616 | tf_op jit(solution)/shard_map/ppermute | solution.py:32
  75.2 2.6 %collective-permute-done.16 = bf16[256,128]{1,0:T(8,128)(2,1)S(1)} collective-permute-done((bf16[256,128]{1,0:T(8,128)(2,1)S(1)}, bf16[256,128]{1,0:T(8,128)(2,1)S(1)}, u32[]{:S(2)}, u32[]{:S(2)}) %collective-permute-start.16) | collective-permute-done | bytes 65568 | tf_op jit(solution)/shard_map/ppermute | solution.py:32
  77.9 3.1 %collective-permute-done.17 = bf16[256,128]{1,0:T(8,128)(2,1)S(1)} collective-permute-done((bf16[256,128]{1,0:T(8,128)(2,1)S(1)}, bf16[256,128]{1,0:T(8,128)(2,1)S(1)}, u32[]{:S(2)}, u32[]{:S(2)}) %collective-permute-start.17) | collective-permute-done | bytes 65568 | tf_op jit(solution)/shard_map/ppermute | solution.py:32
  83.7 3.1 %collective-permute-start.26 = (bf16[2,128,256]{2,1,0:T(8,128)(2,1)S(1)}, bf16[2,128,256]{2,1,0:T(8,128)(2,1)S(1)}, u32[]{:S(2)}, u32[]{:S(2)}) collective-permute-start(bf16[2,128,256]{2,1,0:T(8,128)(2,1)S(1)} %pad_maximum_fusion.2), channel_id=1, source_target_pairs={{0,48},{1,49},{2,50},{3,51},{4,52},{5,53},{6,54},{7,55},{8,56},{9,... | collective-permute-start | bytes 393224 | tf_op jit(solution)/shard_map/ppermute | solution.py:32
  87.9 2.3 %collective-permute-start.19 = (bf16[256,128]{1,0:T(8,128)(2,1)S(1)}, bf16[256,128]{1,0:T(8,128)(2,1)S(1)}, u32[]{:S(2)}, u32[]{:S(2)}) collective-permute-start(bf16[256,128]{1,0:T(8,128)(2,1)S(1)} %add_convert_fusion.4), channel_id=1, source_target_pairs={{0,128},{1,129},{2,130},{3,131},{4,132},{5,133},{6,134},{7,135},{8... | collective-permute-start | bytes 196616 | tf_op jit(solution)/shard_map/ppermute | solution.py:32
  95.4 2.9 %collective-permute-start.22 = (bf16[256,128]{1,0:T(8,128)(2,1)S(1)}, bf16[256,128]{1,0:T(8,128)(2,1)}, u32[]{:S(2)}, u32[]{:S(2)}) collective-permute-start(bf16[256,128]{1,0:T(8,128)(2,1)S(1)} %add_convert_fusion.3.z0), channel_id=1, source_target_pairs={{0,4},{1,5},{2,6},{3,7},{4,0},{5,1},{6,2},{7,3},{8,12},{9,13},{10,... | collective-permute-start | bytes 196616 | tf_op jit(solution)/shard_map/ppermute | solution.py:37
  100.1 2.5 %collective-permute-done.22.z2 = bf16[256,128]{1,0:T(8,128)(2,1)} collective-permute-done((bf16[256,128]{1,0:T(8,128)(2,1)S(1)}, bf16[256,128]{1,0:T(8,128)(2,1)}, u32[]{:S(2)}, u32[]{:S(2)}) %collective-permute-start.22) | collective-permute-done | bytes 65568 | tf_op jit(solution)/shard_map/ppermute | solution.py:37
  105.3 4.7 %top_levels.1 = (f32[128,256]{1,0:T(8,128)S(1)}, bf16[128,256]{1,0:T(8,128)(2,1)S(1)}, f32[2,128,256]{2,1,0:T(8,128)S(1)}, bf16[2,128,256]{2,1,0:T(8,128)(2,1)},...) custom-call(s32[3]{0:T(128)S(1)} %pad_add_fusion.pos, bf16[15,128,1024]{2,1,0:T(8,128)(2,1)} %bitcast.4.own_blocks, ...), custom_call_target="tpu_custom_call" | custom-call | tf_op jit(solution)/shard_map/top_levels/pallas_call | solution.py:239
  112.1 2.7 %collective-permute-start.29 = (bf16[2,128,256]{2,1,0:T(8,128)(2,1)}, bf16[2,128,256]{2,1,0:T(8,128)(2,1)S(1)}, u32[]{:S(2)}, u32[]{:S(2)}) collective-permute-start(bf16[2,128,256]{2,1,0:T(8,128)(2,1)} %get-tuple-element.60), channel_id=1, source_target_pairs={{0,4},{1,5},{2,6},{3,7},{4,0},{5,1},{6,2},{7,3},{8,12},{9,13},{10,... | collective-permute-start | bytes 393224 | tf_op jit(solution)/shard_map/ppermute | solution.py:37
  123.4 4.1 %low_levels.1 = (f32[2,128,256]{2,1,0:T(8,128)S(1)}, bf16[3,128,256]{2,1,0:T(8,128)(2,1)S(1)}, f32[2,128,256]{2,1,0:T(8,128)S(1)}, bf16[2,128,256]{2,1,0:T(8,128...) custom-call(s32[3]{0:T(128)S(1)} %pad_add_fusion.pos, ...), custom_call_target="tpu_custom_call" | custom-call | tf_op jit(solution)/shard_map/low_levels/pallas_call | solution.py:239
  130.3 2.5 %collective-permute-start.33 = (bf16[2,128,256]{2,1,0:T(8,128)(2,1)S(1)}, bf16[2,128,256]{2,1,0:T(8,128)(2,1)S(1)}, u32[]{:S(2)}, u32[]{:S(2)}) collective-permute-start(bf16[2,128,256]{2,1,0:T(8,128)(2,1)S(1)} %get-tuple-element.67), channel_id=1, source_target_pairs={{0,4},{1,5},{2,6},{3,7},{4,0},{5,1},{6,2},{7,3},{8,12},{9,13},{10,... | collective-permute-start | bytes 393224 | tf_op jit(solution)/shard_map/ppermute | solution.py:37
  134.2 2.3 %collective-permute-done.33 = bf16[2,128,256]{2,1,0:T(8,128)(2,1)S(1)} collective-permute-done((bf16[2,128,256]{2,1,0:T(8,128)(2,1)S(1)}, bf16[2,128,256]{2,1,0:T(8,128)(2,1)S(1)}, u32[]{:S(2)}, u32[]{:S(2)}) %collective-permute-start.33) | collective-permute-done | bytes 131104 | tf_op jit(solution)/shard_map/ppermute | solution.py:37
  136.7 14.5 %collective-permute-start.39 = (bf16[3,2,128,128]{3,2,1,0:T(8,128)(2,1)S(1)}, bf16[3,2,128,128]{3,2,1,0:T(8,128)(2,1)S(1)}, u32[]{:S(2)}, u32[]{:S(2)}) collective-permute-start(bf16[3,2,128,128]{3,2,1,0:T(8,128)(2,1)S(1)} %pad_maximum_fusion.1), channel_id=1, source_target_pairs={{0,1},{1,0},{2,3},{3,2},{4,5},{5,4},{6,7},{7,6},{8,9},{9,8},{10,11... | collective-permute-start | bytes 589832 | tf_op jit(solution)/shard_map/ppermute | solution.py:32
  155.1 2.7 %collective-permute-done.37.got3 = bf16[2,128,128]{2,1,0:T(8,128)(2,1)S(1)} collective-permute-done((bf16[2,128,128]{2,1,0:T(8,128)(2,1)S(1)}, bf16[2,128,128]{2,1,0:T(8,128)(2,1)S(1)}, u32[]{:S(2)}, u32[]{:S(2)}) %collective-permute-start.37) | collective-permute-done | bytes 65568 | tf_op jit(solution)/shard_map/ppermute | solution.py:32
  157.8 5.4 %leaf_backward.1 = (f32[1024,512]{1,0:T(8,128)}, f32[5,128,512]{2,1,0:T(8,128)}) custom-call(s32[3]{0:T(128)S(1)} %pad_add_fusion.pos, s32[8,5]{1,0:T(8,128)S(1)} %copy-done.27, bf16[1024,512]{1,0:T(8,128)(2,1)S(1)} %copy-done.4, bf16[8,128,128]{2,1,0:T(8,128)(2,1)S(1)} %copy-done.9, bf16[5,1024,128]{2,1,0:T(8,128)(2,1)S(1)} %bitcast.28, ...), custom_call_target="tpu_custom_call" | custom-call | tf_op jit(solution)/shard_map/leaf_backward/pallas_call | solution.py:239
  (146 shorter events, 62.5 us)
Async XLA Ops:
  7.2 46.0 %all-gather.9.cloned.1.call-start = ((), (), s32[]{:S(2)}) async-start(), calls=%async_computation.1 | async-start | bytes 2359296 | tf_op jit(solution)/shard_map/all_gather | solution.py:268
  9.4 89.4 %all-gather.11.cloned.1.call-start = ((), (), s32[]{:S(2)}) async-start(), calls=%async_computation.2 | async-start | bytes 2359296 | tf_op jit(solution)/shard_map/all_gather | solution.py:268
  10.1 106.6 %all-gather.7.cloned.1.call-start = ((), (), s32[]{:S(2)}) async-start(), calls=%async_computation | async-start | bytes 2359296 | tf_op jit(solution)/shard_map/all_gather | solution.py:268
  14.8 20.4 %collective-permute-start = (bf16[15,128,1024]{2,1,0:T(8,128)(2,1)}, bf16[15,128,1024]{2,1,0:T(8,128)(2,1)}, u32[]{:S(2)}, u32[]{:S(2)}) collective-permute-start(bf16[15,128,1024]{2,1,0:T(8,128)(2,1)} %bitcast.4.own_blocks), channel_id=1, source_target_pairs={{0,1},{1,0},{2,3},{3,2},{4,5},{5,4},{6,7},{7,6},{8,9},{9,8},{10,11... | collective-permute-start | bytes 11796488 | tf_op jit(solution)/shard_map/ppermute | solution.py:32
  18.1 6.6 %collective-permute-start.7 = (bf16[4,2,128,128]{3,2,1,0:T(8,128)(2,1)S(1)}, bf16[4,2,128,128]{3,2,1,0:T(8,128)(2,1)S(1)}, u32[]{:S(2)}, u32[]{:S(2)}) collective-permute-start(bf16[4,2,128,128]{3,2,1,0:T(8,128)(2,1)S(1)} %get-tuple-element.45), channel_id=1, source_target_pairs={{0,1},{1,0},{2,3},{3,2},{4,5},{5,4},{6,7},{7,6},{8,9},{9,8},{10,11... | collective-permute-start | bytes 786440 | tf_op jit(solution)/shard_map/ppermute | solution.py:32
  18.2 6.7 %collective-permute-start.1 = (bf16[128,128]{1,0:T(8,128)(2,1)S(1)}, bf16[128,128]{1,0:T(8,128)(2,1)S(1)}, u32[]{:S(2)}, u32[]{:S(2)}) collective-permute-start(bf16[128,128]{1,0:T(8,128)(2,1)S(1)} %get-tuple-element.40), channel_id=1, source_target_pairs={{0,1},{1,0},{2,3},{3,2},{4,5},{5,4},{6,7},{7,6},{8,9},{9,8},{10,11... | collective-permute-start | bytes 98312 | tf_op jit(solution)/shard_map/ppermute | solution.py:32
  24.8 10.4 %collective-permute-start.8 = (bf16[4,2,128,128]{3,2,1,0:T(8,128)(2,1)S(1)}, bf16[4,2,128,128]{3,2,1,0:T(8,128)(2,1)S(1)}, u32[]{:S(2)}, u32[]{:S(2)}) collective-permute-start(bf16[4,2,128,128]{3,2,1,0:T(8,128)(2,1)S(1)} %pad_maximum_fusion), channel_id=1, source_target_pairs={{0,8},{1,9},{2,10},{3,11},{4,12},{5,13},{6,14},{7,15},{8,0},{9,1},... | collective-permute-start | bytes 786440 | tf_op jit(solution)/shard_map/ppermute | solution.py:32
  26.2 8.9 %collective-permute-start.5 = (bf16[256,128]{1,0:T(8,128)(2,1)S(1)}, bf16[256,128]{1,0:T(8,128)(2,1)S(1)}, u32[]{:S(2)}, u32[]{:S(2)}) collective-permute-start(bf16[256,128]{1,0:T(8,128)(2,1)S(1)} %pad_maximum_fusion.3.z0), channel_id=1, source_target_pairs={{0,4},{1,5},{2,6},{3,7},{4,0},{5,1},{6,2},{7,3},{8,12},{9,13},{10,... | collective-permute-start | bytes 196616 | tf_op jit(solution)/shard_map/ppermute | solution.py:37
  28.9 6.3 %collective-permute-start.6 = (bf16[256,128]{1,0:T(8,128)(2,1)S(1)}, bf16[256,128]{1,0:T(8,128)(2,1)S(1)}, u32[]{:S(2)}, u32[]{:S(2)}) collective-permute-start(bf16[256,128]{1,0:T(8,128)(2,1)S(1)} %pad_maximum_fusion.3.z0), channel_id=1, source_target_pairs={{0,6},{1,7},{2,0},{3,1},{4,2},{5,3},{6,4},{7,5},{8,14},{9,15},{10,... | collective-permute-start | bytes 196616 | tf_op jit(solution)/shard_map/ppermute | solution.py:37
  50.4 6.4 %collective-permute-start.12 = (bf16[2,256,128]{2,1,0:T(8,128)(2,1)S(1)}, bf16[2,256,128]{2,1,0:T(8,128)(2,1)S(1)}, u32[]{:S(2)}, u32[]{:S(2)}) collective-permute-start(bf16[2,256,128]{2,1,0:T(8,128)(2,1)S(1)} %get-tuple-element.49.z0), channel_id=1, source_target_pairs={{0,2},{1,3},{2,4},{3,5},{4,6},{5,7},{6,0},{7,1},{8,10},{9,11},{10,... | collective-permute-start | bytes 393224 | tf_op jit(solution)/shard_map/ppermute | solution.py:37
  50.4 7.1 %collective-permute-start.13 = (bf16[2,256,128]{2,1,0:T(8,128)(2,1)S(1)}, bf16[2,256,128]{2,1,0:T(8,128)(2,1)S(1)}, u32[]{:S(2)}, u32[]{:S(2)}) collective-permute-start(bf16[2,256,128]{2,1,0:T(8,128)(2,1)S(1)} %get-tuple-element.49.z0), channel_id=1, source_target_pairs={{0,4},{1,5},{2,6},{3,7},{4,0},{5,1},{6,2},{7,3},{8,12},{9,13},{10,... | collective-permute-start | bytes 393224 | tf_op jit(solution)/shard_map/ppermute | solution.py:37
  51.8 6.4 %collective-permute-start.14 = (bf16[2,256,128]{2,1,0:T(8,128)(2,1)S(1)}, bf16[2,256,128]{2,1,0:T(8,128)(2,1)S(1)}, u32[]{:S(2)}, u32[]{:S(2)}) collective-permute-start(bf16[2,256,128]{2,1,0:T(8,128)(2,1)S(1)} %get-tuple-element.49.z0), channel_id=1, source_target_pairs={{0,6},{1,7},{2,0},{3,1},{4,2},{5,3},{6,4},{7,5},{8,14},{9,15},{10,... | collective-permute-start | bytes 393224 | tf_op jit(solution)/shard_map/ppermute | solution.py:37
  67.8 7.5 %collective-permute-start.15 = (bf16[256,128]{1,0:T(8,128)(2,1)S(1)}, bf16[256,128]{1,0:T(8,128)(2,1)S(1)}, u32[]{:S(2)}, u32[]{:S(2)}) collective-permute-start(bf16[256,128]{1,0:T(8,128)(2,1)S(1)} %get-tuple-element.51), channel_id=1, source_target_pairs={{0,16},{1,17},{2,18},{3,19},{4,20},{5,21},{6,22},{7,23},{8,24},{9,... | collective-permute-start | bytes 196616 | tf_op jit(solution)/shard_map/ppermute | solution.py:32
  70.9 7.0 %collective-permute-start.16 = (bf16[256,128]{1,0:T(8,128)(2,1)S(1)}, bf16[256,128]{1,0:T(8,128)(2,1)S(1)}, u32[]{:S(2)}, u32[]{:S(2)}) collective-permute-start(bf16[256,128]{1,0:T(8,128)(2,1)S(1)} %get-tuple-element.51), channel_id=1, source_target_pairs={{0,32},{1,33},{2,34},{3,35},{4,36},{5,37},{6,38},{7,39},{8,40},{9,... | collective-permute-start | bytes 196616 | tf_op jit(solution)/shard_map/ppermute | solution.py:32
  81.1 9.2 %collective-permute-start.24 = (bf16[2,128,256]{2,1,0:T(8,128)(2,1)S(1)}, bf16[2,128,256]{2,1,0:T(8,128)(2,1)S(1)}, u32[]{:S(2)}, u32[]{:S(2)}) collective-permute-start(bf16[2,128,256]{2,1,0:T(8,128)(2,1)S(1)} %pad_maximum_fusion.2), channel_id=1, source_target_pairs={{0,16},{1,17},{2,18},{3,19},{4,20},{5,21},{6,22},{7,23},{8,24},{9,... | collective-permute-start | bytes 393224 | tf_op jit(solution)/shard_map/ppermute | solution.py:32
  82.7 8.7 %collective-permute-start.25 = (bf16[2,128,256]{2,1,0:T(8,128)(2,1)S(1)}, bf16[2,128,256]{2,1,0:T(8,128)(2,1)S(1)}, u32[]{:S(2)}, u32[]{:S(2)}) collective-permute-start(bf16[2,128,256]{2,1,0:T(8,128)(2,1)S(1)} %pad_maximum_fusion.2), channel_id=1, source_target_pairs={{0,32},{1,33},{2,34},{3,35},{4,36},{5,37},{6,38},{7,39},{8,40},{9,... | collective-permute-start | bytes 393224 | tf_op jit(solution)/shard_map/ppermute | solution.py:32
  83.7 9.8 %collective-permute-start.26 = (bf16[2,128,256]{2,1,0:T(8,128)(2,1)S(1)}, bf16[2,128,256]{2,1,0:T(8,128)(2,1)S(1)}, u32[]{:S(2)}, u32[]{:S(2)}) collective-permute-start(bf16[2,128,256]{2,1,0:T(8,128)(2,1)S(1)} %pad_maximum_fusion.2), channel_id=1, source_target_pairs={{0,48},{1,49},{2,50},{3,51},{4,52},{5,53},{6,54},{7,55},{8,56},{9,... | collective-permute-start | bytes 393224 | tf_op jit(solution)/shard_map/ppermute | solution.py:32
  86.8 7.5 %collective-permute-start.18 = (bf16[256,128]{1,0:T(8,128)(2,1)S(1)}, bf16[256,128]{1,0:T(8,128)(2,1)S(1)}, u32[]{:S(2)}, u32[]{:S(2)}) collective-permute-start(bf16[256,128]{1,0:T(8,128)(2,1)S(1)} %add_convert_fusion.4), channel_id=1, source_target_pairs={{0,64},{1,65},{2,66},{3,67},{4,68},{5,69},{6,70},{7,71},{8,72},{9,... | collective-permute-start | bytes 196616 | tf_op jit(solution)/shard_map/ppermute | solution.py:32
  87.9 6.4 %collective-permute-start.19 = (bf16[256,128]{1,0:T(8,128)(2,1)S(1)}, bf16[256,128]{1,0:T(8,128)(2,1)S(1)}, u32[]{:S(2)}, u32[]{:S(2)}) collective-permute-start(bf16[256,128]{1,0:T(8,128)(2,1)S(1)} %add_convert_fusion.4), channel_id=1, source_target_pairs={{0,128},{1,129},{2,130},{3,131},{4,132},{5,133},{6,134},{7,135},{8... | collective-permute-start | bytes 196616 | tf_op jit(solution)/shard_map/ppermute | solution.py:32
  91.4 24.4 %collective-permute-start.31 = (bf16[128,256]{1,0:T(8,128)(2,1)}, bf16[128,256]{1,0:T(8,128)(2,1)}, u32[]{:S(2)}, u32[]{:S(2)}) collective-permute-start(bf16[128,256]{1,0:T(8,128)(2,1)} %get-tuple-element.64), channel_id=1, source_target_pairs={{0,16},{1,17},{2,18},{3,19},{4,20},{5,21},{6,22},{7,23},{8,24},{9,... | collective-permute-start | bytes 196616 | tf_op jit(solution)/shard_map/ppermute | solution.py:32
  95.4 7.2 %collective-permute-start.22 = (bf16[256,128]{1,0:T(8,128)(2,1)S(1)}, bf16[256,128]{1,0:T(8,128)(2,1)}, u32[]{:S(2)}, u32[]{:S(2)}) collective-permute-start(bf16[256,128]{1,0:T(8,128)(2,1)S(1)} %add_convert_fusion.3.z0), channel_id=1, source_target_pairs={{0,4},{1,5},{2,6},{3,7},{4,0},{5,1},{6,2},{7,3},{8,12},{9,13},{10,... | collective-permute-start | bytes 196616 | tf_op jit(solution)/shard_map/ppermute | solution.py:37
  112.1 6.7 %collective-permute-start.29 = (bf16[2,128,256]{2,1,0:T(8,128)(2,1)}, bf16[2,128,256]{2,1,0:T(8,128)(2,1)S(1)}, u32[]{:S(2)}, u32[]{:S(2)}) collective-permute-start(bf16[2,128,256]{2,1,0:T(8,128)(2,1)} %get-tuple-element.60), channel_id=1, source_target_pairs={{0,4},{1,5},{2,6},{3,7},{4,0},{5,1},{6,2},{7,3},{8,12},{9,13},{10,... | collective-permute-start | bytes 393224 | tf_op jit(solution)/shard_map/ppermute | solution.py:37
  127.5 9.2 %collective-permute-start.38 = (bf16[3,128,256]{2,1,0:T(8,128)(2,1)S(1)}, bf16[3,128,256]{2,1,0:T(8,128)(2,1)S(1)}, u32[]{:S(2)}, u32[]{:S(2)}) collective-permute-start(bf16[3,128,256]{2,1,0:T(8,128)(2,1)S(1)} %get-tuple-element.71), channel_id=1, source_target_pairs={{0,8},{1,9},{2,10},{3,11},{4,12},{5,13},{6,14},{7,15},{8,0},{9,1},... | collective-permute-start | bytes 589832 | tf_op jit(solution)/shard_map/ppermute | solution.py:32
  136.7 21.1 %collective-permute-start.39 = (bf16[3,2,128,128]{3,2,1,0:T(8,128)(2,1)S(1)}, bf16[3,2,128,128]{3,2,1,0:T(8,128)(2,1)S(1)}, u32[]{:S(2)}, u32[]{:S(2)}) collective-permute-start(bf16[3,2,128,128]{3,2,1,0:T(8,128)(2,1)S(1)} %pad_maximum_fusion.1), channel_id=1, source_target_pairs={{0,1},{1,0},{2,3},{3,2},{4,5},{5,4},{6,7},{7,6},{8,9},{9,8},{10,11... | collective-permute-start | bytes 589832 | tf_op jit(solution)/shard_map/ppermute | solution.py:32
  (47 other events, 260.2 us)
Sparse Core Ops, SparseCore 0:
  9.9 33.5 all-gather.8
  45.9 28.4 all-gather.10
  76.3 28.3 all-gather.6
